TPU v7x, 512 devices: a whole 4x8x8 slice. The times are simulated.
512 devices in a mesh: dp: 16 (over z, core), seq: 32 (over y, x).
Axes of the slice: x: 4, y: 8, z: 8, core: 2. Of those that a mesh axis runs over, the one named last changes fastest.
Arguments:
- bytes_in: bfloat16 [16, 4096, 1024], P('dp', 'seq'), may hold values from -6 to 6
- flags: int32 [16, 4096], P('dp', 'seq'), may hold values from 0 to 1, as said below
- enc_gain: bfloat16 [1024], replicated, may hold values from 0.099609375 to 1.8984375
- conv_weight: bfloat16 [4, 1024], replicated, may hold values from -3 to 3
- widen: bfloat16 [1024], replicated, may hold values from -5 to 5
- main_gain: bfloat16 [2048], replicated, may hold values from 0.099609375 to 1.8984375
- gate_weight: bfloat16 [2048, 4096], P(None, 'seq'), may hold values from -0.125 to 0.125
- up_weight: bfloat16 [2048, 4096], P(None, 'seq'), may hold values from -0.125 to 0.125
- down_weight: bfloat16 [4096, 1024], P('seq'), may hold values from -0.09375 to 0.09375
- out_cot: bfloat16 [16, 4096, 1024], P('dp', 'seq'), may hold values from -6 to 6
Outputs:
- bytes_grad: bfloat16 [16, 4096, 1024], P('dp', 'seq')
- gate_grad: float32 [2048, 4096], P(None, 'seq')
- up_grad: float32 [2048, 4096], P(None, 'seq')
- down_grad: float32 [4096, 1024], P('seq')
Inputs may be any that keep to these rules, and one draw needn't show every extreme that they name: `flags`: every sequence has exactly 512 ones; every device's 128 bytes hold 1 to 48 of them, one device of every sequence exactly 48; the first byte of every sequence is 1.
All inputs are finite; a program needn't handle non-finite values.
Results may differ from a plain program's by a relative error of at most 0.023.
Values may be sent and summed in bfloat16 or wider, within the bound.
A program may use at most 64 MiB of HBM per device.

v0:
```python
import jax
import jax.numpy as jnp
from jax import lax
from jax.sharding import PartitionSpec as P

KW = 4
CAP = 48


EPS = 1e-05


def passed_along(value, axis, steps):
    count = lax.axis_size(axis)
    initial, last = (max(0, -steps), min(count, count - steps))
    return lax.ppermute(value, axis, [(source, source + steps) for source in range(initial, last)])


def rms_scale(value, gain):
    return (
        value
        * lax.rsqrt(jnp.mean(value * value, axis=-1, keepdims=True) + EPS)
        * gain.astype(jnp.float32)
    )


def encode_extended(extended, enc_gain, conv_weight):
    normed = rms_scale(extended, enc_gain)
    length = extended.shape[0] - (KW - 1)
    mixed = conv_weight[0].astype(jnp.float32) * normed[KW - 1 : KW - 1 + length]
    for tap in range(1, KW):
        mixed = (
            mixed
            + conv_weight[tap].astype(jnp.float32) * normed[KW - 1 - tap : KW - 1 - tap + length]
        )
    return extended[KW - 1 :] + jax.nn.silu(mixed)


def main_rows(group_in, group_cot, widen, main_gain, gate_w, up_w, down_w):
    width_in = group_in.shape[1]
    width_all = width_in + widen.shape[0]
    head = group_in.astype(jnp.float32)
    widen32 = widen.astype(jnp.float32)
    gain32 = main_gain.astype(jnp.float32)
    gain_head = gain32[:width_in]
    tail_vec = widen32 * gain32[width_in:]
    square_sum = jnp.sum(head * head, axis=-1, keepdims=True) + jnp.sum(widen32 * widen32)
    inverse = lax.rsqrt(square_sum / width_all + EPS)
    unit_head = head * inverse
    normed_head = unit_head * gain_head
    normed_tail = inverse * tail_vec[None, :]
    normed = jnp.concatenate([normed_head, normed_tail], 1).astype(jnp.bfloat16)
    gate = jnp.dot(normed, gate_w, preferred_element_type=jnp.float32)
    upval = jnp.dot(normed, up_w, preferred_element_type=jnp.float32)
    sigma = jax.nn.sigmoid(gate)
    swish = gate * sigma
    act = (swish * upval).astype(jnp.bfloat16)
    act_cot = jnp.dot(group_cot, down_w.T, preferred_element_type=jnp.float32)
    gate_cot = (act_cot * upval * sigma * (1.0 + gate * (1.0 - sigma))).astype(jnp.bfloat16)
    up_cot = (act_cot * swish).astype(jnp.bfloat16)
    cot_head = jnp.dot(gate_cot, gate_w[:width_in].T, preferred_element_type=jnp.float32)
    cot_head = cot_head + jnp.dot(up_cot, up_w[:width_in].T, preferred_element_type=jnp.float32)
    gate_tail = jnp.dot(
        tail_vec, gate_w[width_in:].astype(jnp.float32), precision=lax.Precision.HIGHEST
    )
    up_tail = jnp.dot(
        tail_vec, up_w[width_in:].astype(jnp.float32), precision=lax.Precision.HIGHEST
    )
    tail_inner = jnp.dot(gate_cot.astype(jnp.float32), gate_tail, precision=lax.Precision.HIGHEST)
    tail_inner = tail_inner + jnp.dot(
        up_cot.astype(jnp.float32), up_tail, precision=lax.Precision.HIGHEST
    )
    scaled_head = cot_head * gain_head
    head_inner = jnp.sum(scaled_head * unit_head, axis=-1, keepdims=True)
    inner = (head_inner + tail_inner[:, None] * inverse) / width_all
    part = (scaled_head - unit_head * inner) * inverse
    return (normed, act, gate_cot, up_cot, part, group_cot)


def row_product(left, right):
    return lax.dot_general(
        left, right, (((0,), (0,)), ((), ())), preferred_element_type=jnp.float32
    )


def body(
    bytes_in,
    flags,
    enc_gain,
    conv_weight,
    widen,
    main_gain,
    gate_weight,
    up_weight,
    down_weight,
    out_cot,
):
    sequence = bytes_in[0]
    cotangent = out_cot[0]
    marks = flags[0]
    byte_count = sequence.shape[0]
    halo_rows = passed_along(sequence[byte_count - (KW - 1) :], "seq", 1)
    extended = jnp.concatenate([halo_rows, sequence], 0).astype(jnp.float32)
    full, pullback = jax.vjp(lambda entry: encode_extended(entry, enc_gain, conv_weight), extended)
    enc_out = full.astype(jnp.bfloat16)
    slot_of = jnp.cumsum(marks) - 1
    count_here = jnp.sum(marks)
    slot_ids = jnp.arange(CAP, dtype=jnp.int32)
    member = slot_of[None, :] == slot_ids[:, None]
    chosen = jnp.logical_and(member, marks[None, :] == 1)
    chosen_bf = chosen.astype(jnp.bfloat16)
    group_in = jnp.dot(chosen_bf, enc_out, preferred_element_type=jnp.float32).astype(jnp.bfloat16)
    leading = (slot_of == -1).astype(jnp.bfloat16)[None, :]
    lead_sum = jnp.dot(leading, cotangent, preferred_element_type=jnp.float32)[0]
    carried = passed_along(lead_sum, "seq", -1)
    own_sums = jnp.dot(member.astype(jnp.bfloat16), cotangent, preferred_element_type=jnp.float32)
    last_slot = (slot_ids == count_here - 1).astype(jnp.float32)[:, None]
    group_cot = (own_sums + last_slot * carried[None, :]).astype(jnp.bfloat16)
    pieces = lax.all_gather((group_in, group_cot), "seq", axis=0, tiled=True)
    results = main_rows(pieces[0], pieces[1], widen, main_gain, gate_weight, up_weight, down_weight)
    normed_all, act_all, gate_cot_all, up_cot_all, part_all, cot_all = results
    widen_cot = lax.psum_scatter(
        part_all.astype(jnp.bfloat16), "seq", scatter_dimension=0, tiled=True
    )
    local_grads = (
        row_product(normed_all, gate_cot_all),
        row_product(normed_all, up_cot_all),
        row_product(act_all, cot_all),
    )
    gate_grad, up_grad, down_grad = (
        lax.psum(local_grads[0].astype(jnp.bfloat16), "dp").astype(jnp.float32),
        lax.psum(local_grads[1].astype(jnp.bfloat16), "dp").astype(jnp.float32),
        lax.psum(local_grads[2].astype(jnp.bfloat16), "dp").astype(jnp.float32),
    )
    group_total = group_cot.astype(jnp.float32) + widen_cot.astype(jnp.float32)
    enc_cot = cotangent.astype(jnp.float32) + jnp.dot(
        chosen.astype(jnp.float32).T, group_total, precision=lax.Precision.HIGHEST
    )
    extended_grad = pullback(enc_cot)[0]
    returned_edge = passed_along(extended_grad[: KW - 1], "seq", -1)
    own_grad = extended_grad[KW - 1 :]
    own_grad = own_grad.at[byte_count - (KW - 1) :].add(returned_edge)
    return (own_grad.astype(jnp.bfloat16)[None], gate_grad, up_grad, down_grad)


def solution(mesh):
    in_specs = (
        P("dp", "seq", None),
        P("dp", "seq"),
        P(),
        P(),
        P(),
        P(),
        P(None, "seq"),
        P(None, "seq"),
        P("seq", None),
        P("dp", "seq", None),
    )
    out_specs = (P("dp", "seq", None), P(None, "seq"), P(None, "seq"), P("seq", None))
    return jax.shard_map(body, mesh=mesh, in_specs=in_specs, out_specs=out_specs, check_vma=False)
```

profile of v0, /device:TPU:1, one launch (start us, length us, event | category | flops | bytes accessed | tf_op | source)
XLA Modules:
  0.0 561.8 jit_solution(6030188092305709720)
XLA Ops:
  7.3 0.8 slice_bitcast_fusion
  8.1 3.9 collective-permute-start.1
  12.1 0.7 compare_bitcast_fusion
  12.7 0.9 slice_convert_fusion.3
  13.6 0.8 copy.17
  14.6 0.7 convert_element_type.95
  15.3 1.1 multiply_reduce_fusion.1
  16.5 1.1 multiply_multiply_fusion
  17.5 0.2 fusion.12
  17.8 1.2 fusion.45
  19.0 0.9 convolution_convert_fusion.3
  20.3 1.3 collective-permute-start
  21.6 0.6 reduce_sum.58
  22.9 1.7 collective-permute-done
  24.6 0.8 add_convert_fusion
  25.6 0.7 fusion.40
  26.2 0.2 convolution_bitcast_fusion
  26.4 0.2 convolution_bitcast_fusion.1
  26.7 79.8 %all-gather.5.cloned.1.call-done = bf16[1536,1024]{1,0:T(8,128)(2,1)} async-done(((bf16[48,1024]{1,0:T(8,128)(2,1)}), bf16[1536,1024]{1,0:T(8,128)(2,1)}) %all-gather.5.cloned.1.call-update) | async-done | bytes 3145744 | tf_op jit(solution)/shard_map/all_gather | solution.py:119
  106.4 2.6 fusion.8
  109.0 0.6 add_rsqrt_fusion
  109.7 2.8 fusion.3
  112.5 2.7 fusion.46
  115.2 2.7 fusion.47
  118.0 73.8 %all-gather.3.cloned.1.call-done = bf16[1536,1024]{1,0:T(8,128)(2,1)} async-done(((bf16[48,1024]{1,0:T(8,128)(2,1)}), bf16[1536,1024]{1,0:T(8,128)(2,1)}) %all-gather.3.cloned.1.call-update) | async-done | bytes 3145744 | tf_op jit(solution)/shard_map/all_gather | solution.py:119
  191.7 3.5 multiply_convert_fusion.2
  195.2 1.0 fusion.23
  196.2 0.4 convolution_reduce_fusion.1
  196.7 0.4 convolution_reduce_fusion
  197.1 0.3 copy-done.1
  197.5 1.5 fusion.4
  199.0 0.6 add_multiply_fusion.2
  199.6 2.6 fusion.7
  202.3 0.2 all-reduce.8.cloned.1.call-start
  202.5 3.7 convolution_convert_fusion.2
  206.2 4.7 convolution_convert_fusion
  211.0 5.3 convolution_convert_fusion.1
  216.3 206.2 %reduce-scatter.2.cloned.1.call-done = bf16[48,1024]{1,0:T(8,128)(2,1)} async-done(((bf16[1536,1024]{1,0:T(8,128)(2,1)}), bf16[48,1024]{1,0:T(8,128)(2,1)}) %reduce-scatter.2.cloned.1.call-update) | async-done | bytes 98320 | tf_op jit(solution)/shard_map/reduce_scatter | solution.py:122
  422.5 1.7 broadcast_multiply_fusion
  424.2 0.2 broadcast_multiply_fusion.1
  424.4 0.4 multiply_reduce_fusion
  424.8 0.3 add_add_fusion
  425.1 1.3 collective-permute-start.2
  426.4 122.0 %all-reduce.8.cloned.1.call-done = (bf16[2048,128]{1,0:T(8,128)(2,1)}, bf16[2048,128]{1,0:T(8,128)(2,1)}, bf16[128,1024]{1,0:T(8,128)(2,1)}) async-done(((bf16[2048,128]{1,0:T(8,128)(2,1)}, bf16[2048,128]{1,0:T(8,128)(2,1)}, bf16[128,1024]{1,0:T(8,128)(2,1)}), (bf16[2048,128]{1,0:T(8,128)(2,1)}, bf16[2048,128]{1,0:T(8,128)(2,1)}, bf16[128,1024]{1,0:T(8,128)(2,1)})) %all-reduce.8.cloned.1.call-update) | async-done | bytes 1310736 | tf_op jit(solution)/shard_map/psum | solution.py:131
  548.4 2.1 convert_element_type.107
  550.5 1.8 convert_element_type.112
  552.3 2.1 convert_element_type.109
  554.6 0.7 copy-done.17
  (62 shorter events, 1.2 us)
Async XLA Ops:
  7.2 184.5 %copy-start = (bf16[128,1024]{1,0:T(8,128)(2,1)S(1)}, bf16[128,1024]{1,0:T(8,128)(2,1)}, u32[]{:S(2)}) copy-start(bf16[128,1024]{1,0:T(8,128)(2,1)} %param.20) | copy-start | bytes 786436
  7.2 14.4 %copy-start.20 = (s32[1,128]{1,0:T(1,128)S(1)}, s32[1,128]{1,0:T(1,128)}, u32[]{:S(2)}) copy-start(s32[1,128]{1,0:T(1,128)} %param.13) | copy-start | bytes 1540
  7.2 12.9 %copy-start.8 = (bf16[1,128,1024]{2,1,0:T(8,128)(2,1)S(1)}, bf16[1,128,1024]{2,1,0:T(8,128)(2,1)}, u32[]{:S(2)}) copy-start(bf16[1,128,1024]{2,1,0:T(8,128)(2,1)} %param.21) | copy-start | bytes 786436
  7.2 18.3 %copy-start.18 = (bf16[2048]{0:T(1024)(128)(2,1)S(1)}, bf16[2048]{0:T(1024)(128)(2,1)}, u32[]{:S(2)}) copy-start(bf16[2048]{0:T(1024)(128)(2,1)} %param.17) | copy-start | bytes 12292
  7.2 18.3 %copy-start.19 = (bf16[1024]{0:T(1024)(128)(2,1)S(1)}, bf16[1024]{0:T(1024)(128)(2,1)}, u32[]{:S(2)}) copy-start(bf16[1024]{0:T(1024)(128)(2,1)} %param.16) | copy-start | bytes 6148
  7.2 19.0 %copy-start.9 = (bf16[2048,128]{1,0:T(8,128)(2,1)S(1)}, bf16[2048,128]{1,0:T(8,128)(2,1)}, u32[]{:S(2)}) copy-start(bf16[2048,128]{1,0:T(8,128)(2,1)} %param.19) | copy-start | bytes 1572868
  7.2 19.2 %copy-start.13 = (bf16[2048,128]{1,0:T(8,128)(2,1)S(1)}, bf16[2048,128]{1,0:T(8,128)(2,1)}, u32[]{:S(2)}) copy-start(bf16[2048,128]{1,0:T(8,128)(2,1)} %param.18) | copy-start | bytes 1572868
  7.2 99.2 %all-gather.5.cloned.1.call-start = ((), (), s32[]{:S(2)}) async-start(), calls=%async_computation.2 | async-start | bytes 3244032 | tf_op jit(solution)/shard_map/all_gather | solution.py:119
  8.1 7.2 %collective-permute-start.1 = (bf16[3,1024]{1,0:T(4,128)(2,1)S(1)}, bf16[3,1024]{1,0:T(4,128)(2,1)S(1)}, u32[]{:S(2)}, u32[]{:S(2)}) collective-permute-start(bf16[3,1024]{1,0:T(4,128)(2,1)S(1)} %slice_bitcast_fusion), channel_id=1, source_target_pairs={{0,1},{1,2},{2,3},{3,4},{4,5},{5,6},{6,7},{7,8},{8,9},{9,10},{10,1... | collective-permute-start | bytes 18440 | tf_op jit(solution)/shard_map/ppermute | solution.py:16
  17.8 1.2 copy-start.12
  20.0 171.7 %all-gather.3.cloned.1.call-start = ((), (), s32[]{:S(2)}) async-start(), calls=%async_computation.1 | async-start | bytes 3244032 | tf_op jit(solution)/shard_map/all_gather | solution.py:119
  20.3 4.3 collective-permute-start
  25.5 397.0 %reduce-scatter.2.cloned.1.call-start = ((), (), s32[]{:S(2)}) async-start(), calls=%async_computation.3 | async-start | bytes 3244032 | tf_op jit(solution)/shard_map/reduce_scatter | solution.py:122
  106.4 6.1 %copy-start.14 = (bf16[2048,128]{1,0:T(8,128)(2,1)S(1)}, bf16[2048,128]{1,0:T(8,128)(2,1)}, u32[]{:S(2)}) copy-start(bf16[2048,128]{1,0:T(8,128)(2,1)} %param.18) | copy-start | bytes 1572868
  112.5 2.8 copy-start.3
  112.5 2.7 copy-start.10
  191.7 3.5 copy-start.15
  195.2 1.5 copy-start.5
  195.2 3.8 copy-start.7
  195.2 2.2 copy-start.1
  195.2 2.3 copy-start.11
  202.3 346.1 %all-reduce.8.cloned.1.call-start = ((), (), s32[]{:S(2)}) async-start(), calls=%async_computation.4 | async-start | bytes 2621440 | tf_op jit(solution)/shard_map/psum | solution.py:131
  206.2 4.7 copy-start.4
  206.2 4.7 copy-start.6
  211.0 211.5 %copy-start.16 = (bf16[48,1024]{1,0:T(8,128)(2,1)S(1)}, bf16[48,1024]{1,0:T(8,128)(2,1)}, u32[]{:S(2)}) copy-start(bf16[48,1024]{1,0:T(8,128)(2,1)} %add_convert_fusion) | copy-start | bytes 294916
  216.2 208.2 %copy-start.2 = (bf16[1,128,1024]{2,1,0:T(8,128)(2,1)S(1)}, bf16[1,128,1024]{2,1,0:T(8,128)(2,1)}, u32[]{:S(2)}) copy-start(bf16[1,128,1024]{2,1,0:T(8,128)(2,1)} %param.12) | copy-start | bytes 786436
  425.1 129.3 %collective-permute-start.2 = (f32[3,1024]{1,0:T(4,128)S(1)}, f32[3,1024]{1,0:T(4,128)S(1)}, u32[]{:S(2)}, u32[]{:S(2)}) collective-permute-start(f32[3,1024]{1,0:T(4,128)S(1)} %slice.106), channel_id=1, source_target_pairs={{1,0},{2,1},{3,2},{4,3},{5,4},{6,5},{7,6},{8,7},{9,8},{10,9},{11,1... | collective-permute-start | bytes 36872 | tf_op jit(solution)/shard_map/ppermute | solution.py:16
  554.6 0.7 copy-start.17
Sparse Core Ops, SparseCore 0:
  20.1 86.2 all-gather.4
  109.6 82.0 all-gather.2
  202.4 220.0 reduce-scatter.1
  425.7 122.6 all-reduce.7
where the time goes:
time: 562 us
  waiting for transfers between devices  484 us (86%)
  matrix products  30 us (5%)
  other arithmetic  23.6 us (4%)
  between operations  14.8 us (3%)
  starting transfers between devices  6.85 us (1%)
    reduce_scatter x1, waiting for transfers between devices, body(): lax.psum_scatter(part_all.astype(jnp.bfloat16), 'seq', scatter_dimension=...  206 us
    all_gather x2, waiting for transfers between devices, body(): pieces = lax.all_gather((group_in, group_cot), 'seq', axis=0, tiled=True)  154 us
    psum x1, waiting for transfers between devices, body(): lax.psum(local_grads[0].astype(jnp.bfloat16), 'dp').astype(jnp.float32)  122 us
    dot_general x3, matrix products, row_product(): lax.dot_general(left, right, (((0,), (0,)), ((), ())), preferred_element_...  13.7 us
  transfers between devices with their start and end apart: 7, of which 5 were waited for; matrix products, arithmetic and copies ran while one was open for 7% of the time, Pallas kernels for 0%

commit v1 on v0

v1 whole, which is shorter than its diff:
```python
import jax
import jax.numpy as jnp
from jax import lax
from jax.experimental import pallas as pl
from jax.experimental.pallas import tpu as pltpu
from jax.sharding import PartitionSpec as P

MESH = pl.DeviceIdType.MESH
F32 = jnp.float32
BF16 = jnp.bfloat16

KW = 4
CAP = 48
EPS = 1e-05
LINE = 4
PARTS = 2
CHUNK = 32

Y_ORDER = (0, -1, 1, -2, 2, -3, 3, 4)
X_ORDER = (0, -1, 1, 2)


def dot(left, right):
    return jnp.dot(left, right, preferred_element_type=F32)


def dot_rows(left, right):
    return lax.dot_general(left, right, (((0,), (0,)), ((), ())), preferred_element_type=F32)


def dot_lanes(left, right):
    return lax.dot_general(left, right, (((1,), (1,)), ((), ())), preferred_element_type=F32)


def kernel(
    params,
    x_ref,
    marks_ref,
    gw_ref,
    uw_ref,
    dw_ref,
    oc_ref,
    bg_ref,
    gg_ref,
    ug_ref,
    dg_ref,
    w_all,
    tails,
    tail_b,
    halo,
    lead_out,
    lead_in,
    norm_x,
    inv_x,
    enc_out,
    slope,
    in_all,
    cot_all,
    normed,
    normed_t,
    cot_t,
    inv_all,
    tin_all,
    act_all,
    cots_all,
    back,
    part_all,
    rs_in,
    v_out,
    v_in,
    v_pair,
    v_sib,
    v_all,
    g_out,
    g_own,
    g_in,
    g_x,
    x_opp,
    x_in,
    h_all,
    z_in,
    final,
    ecot,
    g_mix,
    edge,
    send_sems,
    recv_sems,
):
    n_seq = lax.axis_size("seq")
    n_y = n_seq // LINE
    n_z = lax.axis_size("dp") // 2
    dp = lax.axis_index("dp")
    seq = lax.axis_index("seq")
    z, core = dp // 2, dp % 2
    y, x = seq // LINE, seq % LINE
    width = x_ref.shape[1]
    rows = x_ref.shape[0]
    half = width // 2
    piece = half // PARTS
    z_rows = piece // n_z

    def y_dev(step):
        return {"seq": lax.rem(y + step + n_y, n_y) * LINE + x}

    def x_dev(step):
        return {"seq": y * LINE + lax.rem(x + step + LINE, LINE)}

    def z_dev(step):
        return {"dp": lax.rem(z + step + n_z, n_z) * 2 + core}

    sibling = {"dp": z * 2 + 1 - core}
    after = {"seq": lax.rem(seq + 1, n_seq)}
    before = {"seq": lax.rem(seq + n_seq - 1, n_seq)}

    started = []

    def send(source, target, device):
        index = len(started)
        copy = pltpu.make_async_remote_copy(
            src_ref=source,
            dst_ref=target,
            send_sem=send_sems.at[index],
            recv_sem=recv_sems.at[index],
            device_id=device,
            device_id_type=MESH,
        )
        copy.start()
        started.append(copy)
        return copy

    barrier = pltpu.get_barrier_semaphore()
    peers = [y_dev(step) for step in range(1, n_y)]
    peers += [x_dev(step) for step in range(1, LINE)]
    peers += [z_dev(step) for step in range(1, n_z)]
    peers += [sibling, after, before]
    for peer in peers:
        pl.semaphore_signal(barrier, inc=1, device_id=peer, device_id_type=MESH)

    enc_gain = params[0:1, :]
    taps = [params[1 + tap : 2 + tap, :] for tap in range(KW)]
    widen = params[5:6, :]
    gain_head = params[6:7, :]
    tail_vec = widen * params[7:8, :]
    tail_square = jnp.sum(widen * widen, axis=1, keepdims=True)

    w_all[0, :, 0:128] = gw_ref[0:width, :]
    w_all[0, :, 128:256] = uw_ref[0:width, :]
    w_all[0, :, 256:384] = dw_ref[...].astype(F32).T.astype(BF16)

    marks = marks_ref[...].astype(F32)
    upper = (
        lax.broadcasted_iota(jnp.int32, (rows, rows), 0)
        <= lax.broadcasted_iota(jnp.int32, (rows, rows), 1)
    ).astype(F32).astype(BF16)
    running = dot(jnp.broadcast_to(marks, (16, rows)).astype(BF16), upper)
    lead = jnp.where(running == 0.0, 1.0, 0.0).astype(BF16)
    lead_out[...] = dot(lead, oc_ref[...])[0:8]

    pl.semaphore_wait(barrier, len(peers))

    halo_copy = send(x_ref.at[rows - 16 : rows], halo, after)
    lead_copy = send(lead_out, lead_in, before)

    def w_rows(slot, part):
        start = pl.multiple_of(core * half + part * (half // 2), half // 2)
        return w_all.at[slot, pl.ds(start, half // 2)]

    w_right = [None, None]
    w_left = [None, None]
    for part in (0, 1):
        w_right[part] = send(w_rows(0, part), w_rows(1, part), x_dev(1))
        w_left[1 - part] = send(w_rows(0, 1 - part), w_rows(2, 1 - part), x_dev(-1))

    for r in range(0, rows, CHUNK):
        value = x_ref[r : r + CHUNK].astype(F32)
        inverse = lax.rsqrt(jnp.mean(value * value, axis=1, keepdims=True) + EPS)
        inv_x[r : r + CHUNK] = inverse
        norm_x[16 + r : 16 + r + CHUNK] = value * inverse * enc_gain
    halo_copy.wait_recv()
    value = halo[...].astype(F32) * (seq > 0).astype(F32)
    inverse = lax.rsqrt(jnp.mean(value * value, axis=1, keepdims=True) + EPS)
    norm_x[0:16] = value * inverse * enc_gain
    for r in range(0, rows, CHUNK):
        mixed = taps[0] * norm_x[16 + r : 16 + r + CHUNK]
        for tap in range(1, KW):
            mixed = mixed + taps[tap] * norm_x[16 + r - tap : 16 + r - tap + CHUNK]
        sigma = jax.nn.sigmoid(mixed)
        enc_out[r : r + CHUNK] = (x_ref[r : r + CHUNK].astype(F32) + mixed * sigma).astype(BF16)
        slope[r : r + CHUNK] = sigma * (1.0 + mixed * (1.0 - sigma))

    slot_of = running[0:1] - 1.0
    slot_ids = lax.broadcasted_iota(jnp.int32, (CAP, rows), 0).astype(F32)
    member = jnp.where(slot_ids == slot_of, 1.0, 0.0)
    chosen = (member * marks).astype(BF16)
    in_all[0:CAP] = dot(chosen, enc_out[...]).astype(BF16)

    ring = {}

    def pass_on(which, direction, step):
        buffer = (in_all, cot_all)[which]
        here = Y_ORDER.index(-direction * step)
        there = Y_ORDER.index(4 if step == 3 else -direction * (step + 1))
        ring[which, direction, step] = send(
            buffer.at[here * CAP : (here + 1) * CAP],
            buffer.at[there * CAP : (there + 1) * CAP],
            y_dev(direction),
        )

    pass_on(0, 1, 0)
    pass_on(0, -1, 0)

    own_sums = dot(member.astype(BF16), oc_ref[...])
    lead_copy.wait_recv()
    carried = lead_in[0:1] * (seq < n_seq - 1).astype(F32)
    last_slot = jnp.where(slot_ids[:, 0:1] == running[0:1, rows - 1 : rows] - 1.0, 1.0, 0.0)
    cot_all[0:CAP] = (own_sums + last_slot * carried).astype(BF16)
    pass_on(1, 1, 0)
    pass_on(1, -1, 0)

    w_twin = []

    def swap(slot, part):
        w_twin.append(send(w_rows(slot, part), w_rows(slot, part), sibling))

    w_right[0].wait_recv()
    w_far_a = send(w_rows(1, 0), w_rows(3, 0), x_dev(1))
    w_left[1].wait_recv()
    w_far_b = send(w_rows(2, 1), w_rows(3, 1), x_dev(-1))
    swap(1, 0)
    swap(2, 1)

    tail_b[...] = jnp.broadcast_to(tail_vec, (128, width)).T
    tail_gate = jnp.sum(gw_ref[width : 2 * width].astype(F32) * tail_b[...], axis=0, keepdims=True)
    tail_up = jnp.sum(uw_ref[width : 2 * width].astype(F32) * tail_b[...], axis=0, keepdims=True)
    tails[0, :, 0:128] = jnp.broadcast_to(tail_gate, (8, 128))
    tails[0, :, 128:256] = jnp.broadcast_to(tail_up, (8, 128))
    tail_copies = [
        send(tails.at[0], tails.at[1], x_dev(1)),
        send(tails.at[0], tails.at[2], x_dev(-1)),
        send(tails.at[0], tails.at[3], x_dev(2)),
    ]

    for step in (1, 2):
        for which in (0, 1):
            for direction in (1, -1):
                ring[which, direction, step - 1].wait_recv()
                pass_on(which, direction, step)
        if step == 1:
            w_right[1].wait_recv()
            swap(1, 1)
            w_left[0].wait_recv()
            swap(2, 0)
    w_far_a.wait_recv()
    swap(3, 0)
    w_far_b.wait_recv()
    swap(3, 1)
    ring[0, 1, 2].wait_recv()
    pass_on(0, 1, 3)
    ring[1, -1, 2].wait_recv()
    pass_on(1, -1, 3)
    for copy in tail_copies + w_twin:
        copy.wait_recv()

    def forward(first, last):
        for r in range(first, last, CAP):
            head = in_all[r : r + CAP].astype(F32)
            square = jnp.sum(head * head, axis=1, keepdims=True) + tail_square
            inverse = lax.rsqrt(square / (2 * width) + EPS)
            inv_all[r : r + CAP] = inverse
            normed[r : r + CAP] = (head * inverse * gain_head).astype(BF16)

        tin_all[first:last] = jnp.zeros((last - first, 1), F32)

        def block(slot, carry):
            tail = tails[slot, 0:1, :]
            both = dot(normed[first:last], w_all[slot, :, 0:256]) + inv_all[first:last] * tail
            act_cot = dot(cot_all[first:last], w_all[slot, :, 256:384])
            gate, up = both[:, 0:128], both[:, 128:256]
            sigma = jax.nn.sigmoid(gate)
            swish = gate * sigma
            act_all[slot, first:last, :] = (swish * up).astype(BF16)
            gate_cot = (act_cot * up * sigma * (1.0 + gate * (1.0 - sigma))).astype(BF16)
            up_cot = (act_cot * swish).astype(BF16)
            cots_all[slot, first:last, 0:128] = gate_cot
            cots_all[slot, first:last, 128:256] = up_cot
            tin_all[first:last] += jnp.sum(
                gate_cot.astype(F32) * tail[:, 0:128] + up_cot.astype(F32) * tail[:, 128:256],
                axis=1,
                keepdims=True,
            )
            return carry

        lax.fori_loop(0, LINE, block, 0)

    near = 5 * CAP
    total_rows = len(Y_ORDER) * CAP
    forward(0, near)
    ring[0, -1, 2].wait_recv()
    ring[1, 1, 2].wait_recv()
    ring[0, 1, 3].wait_recv()
    ring[1, -1, 3].wait_recv()
    forward(near, total_rows)

    normed_t[...] = normed[...].T
    cot_t[...] = cot_all[...].T

    def product(start, slot):
        start = pl.multiple_of(start, piece)
        wide = dot(normed_t[pl.ds(start, piece), :], cots_all[slot])
        narrow = dot(cot_t[pl.ds(start, piece), :], act_all[slot])
        return wide, narrow

    pair_copies = []
    for part in range(PARTS):

        def theirs(slot, carry, part=part):
            wide, narrow = product((1 - core) * half + part * piece, slot)
            g_out[part, slot, :, 0:256] = wide.astype(BF16)
            g_out[part, slot, :, 256:384] = narrow.astype(BF16)
            return carry

        lax.fori_loop(0, LINE, theirs, 0)
        pair_copies.append(send(g_out.at[part], g_in.at[part], sibling))

    for part in range(PARTS):

        def ours(slot, carry, part=part):
            wide, narrow = product(core * half + part * piece, slot)
            g_own[part, slot, :, 0:256] = wide
            g_own[part, slot, :, 256:384] = narrow
            return carry

        lax.fori_loop(0, LINE, ours, 0)

    def tail_rows(slot, carry):
        row = jnp.sum(cots_all[slot].astype(F32) * inv_all[...], axis=0, keepdims=True)
        v_out[slot] = jnp.broadcast_to(row, (8, 256))
        return carry

    lax.fori_loop(0, LINE, tail_rows, 0)
    v_copies = [
        send(v_out.at[1], v_in.at[0], x_dev(-1)),
        send(v_out.at[2], v_in.at[1], x_dev(1)),
        send(v_out.at[3], v_in.at[2], x_dev(2)),
    ]

    x_first = []

    def x_start(part):
        pair_copies[part].wait_recv()

        def add(slot, carry):
            g_x[part, slot] = (g_own[part, slot] + g_in[part, slot].astype(F32)).astype(BF16)
            return carry

        lax.fori_loop(1, LINE, add, 0)
        mid = piece // 2
        x_first.append(
            (
                send(g_x.at[part, 3, 0:mid], x_opp.at[part, 0], x_dev(1)),
                send(g_x.at[part, 3, mid:piece], x_opp.at[part, 1], x_dev(-1)),
                send(g_x.at[part, 2, mid:piece], x_in.at[part, 0, mid:piece], x_dev(1)),
                send(g_x.at[part, 1, 0:mid], x_in.at[part, 1, 0:mid], x_dev(-1)),
            )
        )

    rs_copies = []

    def backward(first, last):
        def block(slot, carry):
            back[first:last] += dot_lanes(cots_all[slot, first:last], w_all[slot, :, 0:256])
            return carry

        back[first:last] = dot_lanes(cots_all[0, first:last], w_all[0, :, 0:256])
        lax.fori_loop(1, LINE, block, 0)
        for r in range(first, last, CAP):
            inverse = inv_all[r : r + CAP]
            unit = in_all[r : r + CAP].astype(F32) * inverse
            scaled = back[r : r + CAP] * gain_head
            inner = jnp.sum(scaled * unit, axis=1, keepdims=True) + tin_all[r : r + CAP] * inverse
            part_all[r : r + CAP] = (
                (scaled - unit * (inner / (2 * width))) * inverse
            ).astype(BF16)
            step = Y_ORDER[r // CAP]
            if step:
                there = Y_ORDER.index(4 if step == 4 else -step)
                rs_copies.append(
                    send(part_all.at[r : r + CAP], rs_in.at[there], y_dev(step))
                )

    backward(4 * CAP, 8 * CAP)
    x_start(0)
    backward(0, 4 * CAP)
    x_start(1)

    for copy in v_copies:
        copy.wait_recv()
    v_pair[...] = v_out[0] + v_in[0] + v_in[1] + v_in[2]
    v_swap = send(v_pair, v_sib, sibling)

    x_second = []
    mid = piece // 2
    for part in range(PARTS):
        x_first[part][0].wait_recv()
        g_x[part, 2, 0:mid] = (
            g_x[part, 2, 0:mid].astype(F32) + x_opp[part, 0].astype(F32)
        ).astype(BF16)
        second_a = send(g_x.at[part, 2, 0:mid], x_in.at[part, 0, 0:mid], x_dev(1))
        x_first[part][1].wait_recv()
        g_x[part, 1, mid:piece] = (
            g_x[part, 1, mid:piece].astype(F32) + x_opp[part, 1].astype(F32)
        ).astype(BF16)
        second_b = send(g_x.at[part, 1, mid:piece], x_in.at[part, 1, mid:piece], x_dev(-1))
        x_second.append((second_a, second_b))

    v_swap.wait_recv()
    v_all[z] = v_pair[...] + v_sib[...]
    v_spread = [send(v_all.at[z], v_all.at[z], z_dev(step)) for step in range(1, n_z)]

    z_first = []
    for part in range(PARTS):
        for copy in x_first[part][2:] + x_second[part]:
            copy.wait_recv()
        h_all[part] = (
            g_own[part, 0]
            + g_in[part, 0].astype(F32)
            + x_in[part, 0].astype(F32)
            + x_in[part, 1].astype(F32)
        ).astype(BF16)
        copies = []
        for step in range(1, n_z):
            start = pl.multiple_of(lax.rem(z + step, n_z) * z_rows, z_rows)
            copies.append(
                send(h_all.at[part, pl.ds(start, z_rows)], z_in.at[part, step - 1], z_dev(step))
            )
        z_first.append(copies)

    for copy in rs_copies:
        copy.wait_recv()
    widen_cot = part_all[0:CAP].astype(F32)
    for slot in range(1, len(Y_ORDER)):
        widen_cot = widen_cot + rs_in[slot].astype(F32)
    spread = dot_rows(chosen, cot_all[0:CAP]) + dot_rows(chosen, widen_cot.astype(BF16))
    ecot[...] = oc_ref[...].astype(F32) + spread
    for r in range(0, rows, CHUNK):
        g_mix[r : r + CHUNK] = ecot[r : r + CHUNK] * slope[r : r + CHUNK]
    edge_copy = send(g_mix.at[0:8], edge, before)

    z_second = []
    for part in range(PARTS):
        own = pl.multiple_of(z * z_rows, z_rows)
        total = h_all[part, pl.ds(own, z_rows)].astype(F32)
        for step in range(1, n_z):
            z_first[part][step - 1].wait_recv()
            total = total + z_in[part, step - 1].astype(F32)
        start = pl.multiple_of(core * half + part * piece + z * z_rows, z_rows)
        final[pl.ds(start, z_rows)] = total.astype(BF16)
        mine = final.at[pl.ds(start, z_rows)]
        z_second.append([send(mine, mine, z_dev(step)) for step in range(1, n_z)])

    edge_copy.wait_recv()
    g_mix[rows : rows + 8] = edge[...] * (seq < n_seq - 1).astype(F32)
    for r in range(0, rows, CHUNK):
        grad = taps[0] * g_mix[r : r + CHUNK]
        for tap in range(1, KW):
            grad = grad + taps[tap] * g_mix[r + tap : r + tap + CHUNK]
        grad = grad * enc_gain
        value = x_ref[r : r + CHUNK].astype(F32)
        inverse = inv_x[r : r + CHUNK]
        inner = jnp.mean(grad * value, axis=1, keepdims=True) * (inverse * inverse)
        bg_ref[r : r + CHUNK] = (
            ecot[r : r + CHUNK] + (grad - value * inner) * inverse
        ).astype(BF16)

    for copy in v_spread:
        copy.wait_recv()
    v_total = v_all[0]
    for chip in range(1, n_z):
        v_total = v_total + v_all[chip]
    gg_ref[width : 2 * width] = tail_b[...] * v_total[0:1, 0:128]
    ug_ref[width : 2 * width] = tail_b[...] * v_total[0:1, 128:256]

    last_copies = []
    for part in range(PARTS):
        for copy in z_second[part]:
            copy.wait_recv()
        start = pl.multiple_of(core * half + part * piece, piece)
        mine = final.at[pl.ds(start, piece)]
        last_copies.append(send(mine, mine, sibling))
    for copy in last_copies:
        copy.wait_recv()
    gg_ref[0:width] = final[:, 0:128].astype(F32)
    ug_ref[0:width] = final[:, 128:256].astype(F32)
    dg_ref[...] = final[:, 256:384].astype(F32).T

    for copy in started:
        copy.wait_send()


def body(
    bytes_in,
    flags,
    enc_gain,
    conv_weight,
    widen,
    main_gain,
    gate_weight,
    up_weight,
    down_weight,
    out_cot,
):
    rows, width = bytes_in.shape[1:]
    n_y = lax.axis_size("seq") // LINE
    n_z = lax.axis_size("dp") // 2
    assert n_y == len(Y_ORDER)
    piece = width // 2 // PARTS
    groups = n_y * CAP
    params = jnp.concatenate(
        [enc_gain[None], conv_weight, widen[None], main_gain.reshape(2, width)], 0
    ).astype(F32)
    vmem = pl.BlockSpec(memory_space=pltpu.VMEM)
    scratch = [
        ((LINE, width, 384), BF16),
        ((LINE, 8, 256), F32),
        ((width, 128), F32),
        ((16, width), BF16),
        ((8, width), F32),
        ((8, width), F32),
        ((rows + 16, width), F32),
        ((rows, 1), F32),
        ((rows, width), BF16),
        ((rows, width), F32),
        ((groups, width), BF16),
        ((groups, width), BF16),
        ((groups, width), BF16),
        ((width, groups), BF16),
        ((width, groups), BF16),
        ((groups, 1), F32),
        ((groups, 1), F32),
        ((LINE, groups, 128), BF16),
        ((LINE, groups, 256), BF16),
        ((groups, width), F32),
        ((groups, width), BF16),
        ((n_y, CAP, width), BF16),
        ((LINE, 8, 256), F32),
        ((LINE - 1, 8, 256), F32),
        ((8, 256), F32),
        ((8, 256), F32),
        ((n_z, 8, 256), F32),
        ((PARTS, LINE, piece, 384), BF16),
        ((PARTS, LINE, piece, 384), F32),
        ((PARTS, LINE, piece, 384), BF16),
        ((PARTS, LINE, piece, 384), BF16),
        ((PARTS, 2, piece // 2, 384), BF16),
        ((PARTS, 2, piece, 384), BF16),
        ((PARTS, piece, 384), BF16),
        ((PARTS, n_z - 1, piece // n_z, 384), BF16),
        ((width, 384), BF16),
        ((rows, width), F32),
        ((rows + 8, width), F32),
        ((8, width), F32),
    ]
    outs = pl.pallas_call(
        kernel,
        out_shape=(
            jax.ShapeDtypeStruct((rows, width), BF16),
            jax.ShapeDtypeStruct((2 * width, 128), F32),
            jax.ShapeDtypeStruct((2 * width, 128), F32),
            jax.ShapeDtypeStruct((128, width), F32),
        ),
        in_specs=[vmem] * 7,
        out_specs=[vmem] * 4,
        scratch_shapes=[pltpu.VMEM(shape, kind) for shape, kind in scratch]
        + [pltpu.SemaphoreType.DMA((112,)), pltpu.SemaphoreType.DMA((112,))],
        compiler_params=pltpu.CompilerParams(
            collective_id=0, has_side_effects=True, vmem_limit_bytes=48 * 1024 * 1024
        ),
    )(params, bytes_in[0], flags, gate_weight, up_weight, down_weight, out_cot[0])
    return (outs[0][None], outs[1], outs[2], outs[3])


def solution(mesh):
    in_specs = (
        P("dp", "seq", None),
        P("dp", "seq"),
        P(),
        P(),
        P(),
        P(),
        P(None, "seq"),
        P(None, "seq"),
        P("seq", None),
        P("dp", "seq", None),
    )
    out_specs = (P("dp", "seq", None), P(None, "seq"), P(None, "seq"), P("seq", None))
    return jax.shard_map(body, mesh=mesh, in_specs=in_specs, out_specs=out_specs, check_vma=False)
```

time: 562 us -> 91.4 us (0.16)
  waiting for transfers between devices: 484 us -> 0 us
  Pallas kernels: 0 us -> 78.2 us
  matrix products: 30 us -> 0 us
  other arithmetic: 23.6 us -> 0.02 us
  between operations: 14.8 us -> 0.67 us
  local copies, waits for them, and re-layouts: 2.98 us -> 11 us
  starting transfers between devices: 6.85 us -> 0 us
    reduce_scatter x1 -> x0, waiting for transfers between devices: 206 us -> none  [body(): lax.psum_scatter(part_all.astype(jnp.bfloat16), 'seq', scatter_dimension=...]
    all_gather x2 -> x0, waiting for transfers between devices: 154 us -> none  [body(): pieces = lax.all_gather((group_in, group_cot), 'seq', axis=0, tiled=True)]
    psum x1 -> x0, waiting for transfers between devices: 122 us -> none  [body(): lax.psum(local_grads[0].astype(jnp.bfloat16), 'dp').astype(jnp.float32)]
    pallas_call x0 -> x1, Pallas kernels: none -> 78.2 us  [body(): pl.pallas_call(kernel, out_shape=(jax.ShapeDtypeStruct((rows, width), BF1...]
    dot_general x16 -> x0, matrix products: 30 us -> none  [the longest x3 13.7 us: row_product(): lax.dot_general(left, right, (((0,), (0,)), ((), ())), preferred_element_...]
    convert_element_type x8 -> x1, other arithmetic: 10.5 us -> 0.02 us  [body(): params = jnp.concatenate([enc_gain[None], conv_weight, widen[None], main_...]
    unnamed x42 -> x24, local copies, waits for them, and re-layouts: 1.17 us -> 11 us
    ppermute x3 -> x0, starting transfers between devices: 6.51 us -> none  [passed_along(): lax.ppermute(value, axis, [(source, source + steps) for source in range(i...]
  transfers between devices with their start and end apart: 7 -> 0, of which waited for: 5 -> 0; matrix products, arithmetic and copies ran while one was open for 7% -> 0% of each run, Pallas kernels for 0% -> 0%
where the time goes in v1:
time: 91.4 us; the launch traced here: 90 us
  Pallas kernels  78.2 us (86%)
  local copies, waits for them, and re-layouts  11 us (12%)
    pallas_call x1, Pallas kernels, body(): pl.pallas_call(kernel, out_shape=(jax.ShapeDtypeStruct((rows, width), BF1...  78.2 us
    unnamed x24, local copies, waits for them, and re-layouts  11 us

profile of v1, /device:TPU:1, one launch (start us, length us, event | category | flops | bytes accessed | tf_op | source)
XLA Modules:
  0.0 90.0 jit_solution(11251632788817944533)
XLA Ops:
  0.6 0.0 copy-start.8
  0.6 0.7 copy-done.8
  1.3 0.0 copy-start.9
  1.3 0.0 copy-start.7
  1.3 0.7 copy-done.9
  2.0 0.0 copy-start.6
  2.0 0.0 copy-done.7
  2.0 0.7 copy-done.6
  2.7 0.0 copy-start.5
  2.7 0.6 copy-done.5
  3.3 0.0 copy-start
  3.4 1.0 %copy-done = bf16[2048,128]{1,0:T(8,128)(2,1)S(1)} copy-done((bf16[2048,128]{1,0:T(8,128)(2,1)S(1)}, bf16[2048,128]{1,0:T(8,128)(2,1)}, u32[]{:S(2)}) %copy-start) | copy-done | bytes 524312
  4.4 0.0 copy-start.1
  4.4 1.0 %copy-done.1 = bf16[2048,128]{1,0:T(8,128)(2,1)S(1)} copy-done((bf16[2048,128]{1,0:T(8,128)(2,1)S(1)}, bf16[2048,128]{1,0:T(8,128)(2,1)}, u32[]{:S(2)}) %copy-start.1) | copy-done | bytes 524312
  5.4 0.0 copy-start.2
  5.4 0.9 %copy-done.2 = bf16[1,128,1024]{2,1,0:T(8,128)(2,1)S(1)} copy-done((bf16[1,128,1024]{2,1,0:T(8,128)(2,1)S(1)}, bf16[1,128,1024]{2,1,0:T(8,128)(2,1)}, u32[]{:S(2)}) %copy-start.2) | copy-done | bytes 262168
  6.4 0.0 copy-start.3
  6.4 0.9 %copy-done.3 = bf16[128,1024]{1,0:T(8,128)(2,1)S(1)} copy-done((bf16[128,1024]{1,0:T(8,128)(2,1)S(1)}, bf16[128,1024]{1,0:T(8,128)(2,1)}, u32[]{:S(2)}) %copy-start.3) | copy-done | bytes 262168
  7.3 0.0 copy-start.4
  7.3 0.9 %copy-done.4 = bf16[1,128,1024]{2,1,0:T(8,128)(2,1)S(1)} copy-done((bf16[1,128,1024]{2,1,0:T(8,128)(2,1)S(1)}, bf16[1,128,1024]{2,1,0:T(8,128)(2,1)}, u32[]{:S(2)}) %copy-start.4) | copy-done | bytes 262168
  8.3 78.2 %shard_map.129 = (bf16[128,1024]{1,0:T(8,128)(2,1)S(1)}, f32[2048,128]{1,0:T(8,128)S(1)}, f32[2048,128]{1,0:T(8,128)S(1)}, f32[128,1024]{1,0:T(8,128)S(1)}) custom-call(f32[8,1024]{1,0:T(8,128)S(1)} %maximum_convert_fusion.params, bf16[128,1024]{1,0:T(8,128)(2,1)S(1)} %bitcast.4, s32[1,128]{1,0:T(1,128)S(1)} %copy-done.5, bf16[2048,128]{1,0:T(8,128)(2,1)S(1)} %copy-done, ...), custom_call_target="tpu_custom_call" | custom-call | tf_op jit(solution)/shard_map/pallas_call | solution.py:563
  86.5 0.7 copy.18
  87.2 1.0 %copy.19 = f32[2048,128]{1,0:T(8,128)} copy(f32[2048,128]{1,0:T(8,128)S(1)} %get-tuple-element.17) | data formatting | bytes 2097152
  88.2 1.0 %copy.20 = f32[2048,128]{1,0:T(8,128)} copy(f32[2048,128]{1,0:T(8,128)S(1)} %get-tuple-element.18) | data formatting | bytes 2097152
  89.2 0.8 copy.21
  (4 shorter events, 0.0 us)
Async XLA Ops:
  0.6 0.7 copy-start.8
  1.3 0.7 copy-start.9
  1.3 0.7 copy-start.7
  2.0 0.7 copy-start.6
  2.7 0.7 copy-start.5
  3.3 1.0 %copy-start = (bf16[2048,128]{1,0:T(8,128)(2,1)S(1)}, bf16[2048,128]{1,0:T(8,128)(2,1)}, u32[]{:S(2)}) copy-start(bf16[2048,128]{1,0:T(8,128)(2,1)} %gw_ref.1) | copy-start | bytes 1572868
  4.4 1.0 %copy-start.1 = (bf16[2048,128]{1,0:T(8,128)(2,1)S(1)}, bf16[2048,128]{1,0:T(8,128)(2,1)}, u32[]{:S(2)}) copy-start(bf16[2048,128]{1,0:T(8,128)(2,1)} %uw_ref.1) | copy-start | bytes 1572868
  5.4 0.9 %copy-start.2 = (bf16[1,128,1024]{2,1,0:T(8,128)(2,1)S(1)}, bf16[1,128,1024]{2,1,0:T(8,128)(2,1)}, u32[]{:S(2)}) copy-start(bf16[1,128,1024]{2,1,0:T(8,128)(2,1)} %param.10) | copy-start | bytes 786436
  6.4 0.9 %copy-start.3 = (bf16[128,1024]{1,0:T(8,128)(2,1)S(1)}, bf16[128,1024]{1,0:T(8,128)(2,1)}, u32[]{:S(2)}) copy-start(bf16[128,1024]{1,0:T(8,128)(2,1)} %dw_ref.1) | copy-start | bytes 786436
  7.3 0.9 %copy-start.4 = (bf16[1,128,1024]{2,1,0:T(8,128)(2,1)S(1)}, bf16[1,128,1024]{2,1,0:T(8,128)(2,1)}, u32[]{:S(2)}) copy-start(bf16[1,128,1024]{2,1,0:T(8,128)(2,1)} %param.19) | copy-start | bytes 786436

commit v2 on v1

v2 whole, which is shorter than its diff:
```python
import jax
import jax.numpy as jnp
from jax import lax
from jax.experimental import pallas as pl
from jax.experimental.pallas import tpu as pltpu
from jax.sharding import PartitionSpec as P

MESH = pl.DeviceIdType.MESH
F32 = jnp.float32
BF16 = jnp.bfloat16

KW = 4
CAP = 48
EPS = 1e-05
LINE = 4
PARTS = 4
CHUNK = 32

Y_ORDER = (0, -1, 1, -2, 2, -3, 3, 4)
Y_ROW = (0, 48, 96, 144, 192, 256, 304, 352)
NEAR = (0, 240)
FAR = (256, 400)
ROWS = 512
X_ORDER = (0, -1, 1, 2)


def dot(left, right):
    return jnp.dot(left, right, preferred_element_type=F32)


def dot_rows(left, right):
    return lax.dot_general(left, right, (((0,), (0,)), ((), ())), preferred_element_type=F32)


def dot_lanes(left, right):
    return lax.dot_general(left, right, (((1,), (1,)), ((), ())), preferred_element_type=F32)


def as_row(value):
    value = value.astype(F32)
    return jnp.concatenate([value[i : i + 1] for i in range(value.shape[0])], axis=1)


def kernel(
    x_hbm,
    marks_hbm,
    enc_gain_hbm,
    conv_hbm,
    widen_hbm,
    main_gain_hbm,
    gw_hbm,
    uw_hbm,
    dw_hbm,
    oc_hbm,
    bg_ref,
    final,
    tail_b,
    v_ref,
    x_ref,
    marks_ref,
    enc_gain_ref,
    conv_ref,
    widen_ref,
    main_gain_ref,
    gw_tail,
    uw_tail,
    dw_ref,
    oc_ref,
    w_all,
    tails,
    halo,
    lead_out,
    lead_in,
    norm_x,
    inv_x,
    enc_out,
    slope,
    in_all,
    cot_all,
    normed,
    normed_t,
    cot_t,
    inv_all,
    tin_all,
    act_all,
    cots_all,
    back,
    part_all,
    y_in,
    y_relay,
    y_cross,
    y_mid,
    v_out,
    v_in,
    v_pair,
    v_sib,
    v_all,
    g_acc,
    g_out,
    g_in,
    g_x,
    x_opp,
    x_in,
    h_all,
    z_in,
    z_relay,
    z_cross,
    z_mid,
    ecot,
    g_mix,
    edge,
    load_sems,
    send_sems,
    recv_sems,
):
    n_seq = lax.axis_size("seq")
    n_y = n_seq // LINE
    n_z = lax.axis_size("dp") // 2
    dp = lax.axis_index("dp")
    seq = lax.axis_index("seq")
    z, core = dp // 2, dp % 2
    y, x = seq // LINE, seq % LINE
    rows, width = x_ref.shape
    half = width // 2
    piece = half // PARTS
    mid = piece // 2
    z_rows = piece // n_z

    def y_dev(step):
        return {"seq": lax.rem(y + step + n_y, n_y) * LINE + x}

    def x_dev(step):
        return {"seq": y * LINE + lax.rem(x + step + LINE, LINE)}

    def z_dev(step):
        return {"dp": lax.rem(z + step + n_z, n_z) * 2 + core}

    sibling = {"dp": z * 2 + 1 - core}
    after = {"seq": lax.rem(seq + 1, n_seq)}
    before = {"seq": lax.rem(seq + n_seq - 1, n_seq)}

    loads = []

    def load(source, target):
        copy = pltpu.make_async_copy(source, target, load_sems.at[len(loads)])
        copy.start()
        loads.append(copy)
        return copy

    load_marks = load(marks_hbm, marks_ref)
    load_oc = load(oc_hbm, oc_ref)
    load_x = load(x_hbm, x_ref)
    load_gain = load(enc_gain_hbm, enc_gain_ref)
    load_conv = load(conv_hbm, conv_ref)
    load_w = [
        load(dw_hbm, dw_ref),
        load(gw_hbm.at[0:width], w_all.at[0, :, 0:128]),
        load(uw_hbm.at[0:width], w_all.at[0, :, 128:256]),
    ]
    load_tail = [
        load(widen_hbm, widen_ref),
        load(main_gain_hbm, main_gain_ref),
        load(gw_hbm.at[width : 2 * width], gw_tail),
        load(uw_hbm.at[width : 2 * width], uw_tail),
    ]

    started = []

    def send(source, target, device):
        index = len(started)
        copy = pltpu.make_async_remote_copy(
            src_ref=source,
            dst_ref=target,
            send_sem=send_sems.at[index],
            recv_sem=recv_sems.at[index],
            device_id=device,
            device_id_type=MESH,
        )
        copy.start()
        started.append(copy)
        return copy

    barrier = pltpu.get_barrier_semaphore()
    peers = [y_dev(step) for step in (1, -1, 2, -2)]
    peers += [x_dev(step) for step in (1, -1, 2)]
    peers += [z_dev(step) for step in range(1, n_z)]
    peers += [sibling, after, before]
    for peer in peers:
        pl.semaphore_signal(barrier, inc=1, device_id=peer, device_id_type=MESH)

    load_marks.wait()
    marks = marks_ref[...].astype(F32)
    upper = (
        lax.broadcasted_iota(jnp.int32, (rows, rows), 0)
        <= lax.broadcasted_iota(jnp.int32, (rows, rows), 1)
    ).astype(F32).astype(BF16)
    running = dot(jnp.broadcast_to(marks, (16, rows)).astype(BF16), upper)
    lead = jnp.where(running == 0.0, 1.0, 0.0).astype(BF16)
    slot_ids = lax.broadcasted_iota(jnp.int32, (CAP, rows), 0).astype(F32)
    member = jnp.where(slot_ids == running[0:1] - 1.0, 1.0, 0.0)
    chosen = (member * marks).astype(BF16)
    last_slot = jnp.where(slot_ids[:, 0:1] == running[0:1, rows - 1 : rows] - 1.0, 1.0, 0.0)
    load_oc.wait()
    lead_out[...] = dot(lead, oc_ref[...])[0:8]

    pl.semaphore_wait(barrier, len(peers))

    halo_copy = send(x_hbm.at[rows - 16 : rows], halo, after)
    lead_copy = send(lead_out, lead_in, before)
    own_sums = dot(member.astype(BF16), oc_ref[...])

    for copy in load_w:
        copy.wait()
    w_all[0, :, 256:384] = dw_ref[...].astype(F32).T.astype(BF16)

    def w_rows(slot, part):
        start = pl.multiple_of(core * half + part * (half // 2), half // 2)
        return w_all.at[slot, pl.ds(start, half // 2)]

    w_right = [None, None]
    w_left = [None, None]
    for part in (0, 1):
        w_right[part] = send(w_rows(0, part), w_rows(1, part), x_dev(1))
        w_left[1 - part] = send(w_rows(0, 1 - part), w_rows(2, 1 - part), x_dev(-1))

    ring = {}

    def pass_on(which, direction, step):
        buffer = (in_all, cot_all)[which]
        here = Y_ROW[Y_ORDER.index(-direction * step)]
        there = Y_ROW[Y_ORDER.index(4 if step == 3 else -direction * (step + 1))]
        ring[which, direction, step] = send(
            buffer.at[here : here + CAP], buffer.at[there : there + CAP], y_dev(direction)
        )

    lead_copy.wait_recv()
    carried = lead_in[0:1] * (seq < n_seq - 1).astype(F32)
    cot_all[0:CAP] = (own_sums + last_slot * carried).astype(BF16)
    pass_on(1, 1, 0)
    pass_on(1, -1, 0)

    load_gain.wait()
    load_conv.wait()
    load_x.wait()
    enc_gain = as_row(enc_gain_ref[...])
    taps = [conv_ref[tap : tap + 1, :].astype(F32) for tap in range(KW)]
    for r in range(0, rows, CHUNK):
        value = x_ref[r : r + CHUNK].astype(F32)
        inverse = lax.rsqrt(jnp.mean(value * value, axis=1, keepdims=True) + EPS)
        inv_x[r : r + CHUNK] = inverse
        norm_x[16 + r : 16 + r + CHUNK] = value * inverse * enc_gain
    halo_copy.wait_recv()
    value = halo[...].astype(F32) * (seq > 0).astype(F32)
    inverse = lax.rsqrt(jnp.mean(value * value, axis=1, keepdims=True) + EPS)
    norm_x[0:16] = value * inverse * enc_gain
    for r in range(0, rows, CHUNK):
        mixed = taps[0] * norm_x[16 + r : 16 + r + CHUNK]
        for tap in range(1, KW):
            mixed = mixed + taps[tap] * norm_x[16 + r - tap : 16 + r - tap + CHUNK]
        sigma = jax.nn.sigmoid(mixed)
        enc_out[r : r + CHUNK] = (x_ref[r : r + CHUNK].astype(F32) + mixed * sigma).astype(BF16)
        slope[r : r + CHUNK] = sigma * (1.0 + mixed * (1.0 - sigma))
    in_all[0:CAP] = dot(chosen, enc_out[...]).astype(BF16)
    pass_on(0, 1, 0)
    pass_on(0, -1, 0)

    w_twin = []

    def swap(slot, part):
        w_twin.append(send(w_rows(slot, part), w_rows(slot, part), sibling))

    w_right[0].wait_recv()
    w_far_a = send(w_rows(1, 0), w_rows(3, 0), x_dev(1))
    w_left[1].wait_recv()
    w_far_b = send(w_rows(2, 1), w_rows(3, 1), x_dev(-1))
    swap(1, 0)
    swap(2, 1)

    for copy in load_tail:
        copy.wait()
    widen = as_row(widen_ref[...])
    main_gain = as_row(main_gain_ref[...])
    gain_head = main_gain[:, 0:width]
    tail_vec = widen * main_gain[:, width : 2 * width]
    tail_square = jnp.sum(widen * widen, axis=1, keepdims=True)
    tail_b[...] = jnp.broadcast_to(tail_vec, (128, width)).T
    tail_gate = jnp.sum(gw_tail[...].astype(F32) * tail_b[...], axis=0, keepdims=True)
    tail_up = jnp.sum(uw_tail[...].astype(F32) * tail_b[...], axis=0, keepdims=True)
    tails[0, :, 0:128] = jnp.broadcast_to(tail_gate, (8, 128))
    tails[0, :, 128:256] = jnp.broadcast_to(tail_up, (8, 128))
    tail_copies = [
        send(tails.at[0], tails.at[1], x_dev(1)),
        send(tails.at[0], tails.at[2], x_dev(-1)),
        send(tails.at[0], tails.at[3], x_dev(2)),
    ]

    def relay(step):
        for which in (1, 0):
            for direction in (1, -1):
                ring[which, direction, step - 1].wait_recv()
                pass_on(which, direction, step)

    relay(1)
    w_right[1].wait_recv()
    swap(1, 1)
    w_left[0].wait_recv()
    swap(2, 0)
    for first, last in ((NEAR[1], FAR[0]), (FAR[1], ROWS)):
        count = last - first
        normed[first:last] = jnp.zeros((count, width), BF16)
        cot_all[first:last] = jnp.zeros((count, width), BF16)
        inv_all[first:last] = jnp.zeros((count, 1), F32)
        act_all[:, first:last] = jnp.zeros((LINE, count, 128), BF16)
        cots_all[:, first:last] = jnp.zeros((LINE, count, 256), BF16)
    relay(2)

    def normalise(first, last):
        for r in range(first, last, CAP):
            head = in_all[r : r + CAP].astype(F32)
            square = jnp.sum(head * head, axis=1, keepdims=True) + tail_square
            inverse = lax.rsqrt(square / (2 * width) + EPS)
            inv_all[r : r + CAP] = inverse
            normed[r : r + CAP] = (head * inverse * gain_head).astype(BF16)
        tin_all[first:last] = jnp.zeros((last - first, 1), F32)

    def forward(first, last, low, high):
        def block(slot, carry):
            tail = tails[slot, 0:1, :]
            both = dot(normed[first:last], w_all[slot, :, 0:256]) + inv_all[first:last] * tail
            act_cot = dot(cot_all[first:last], w_all[slot, :, 256:384])
            gate, up = both[:, 0:128], both[:, 128:256]
            sigma = jax.nn.sigmoid(gate)
            swish = gate * sigma
            act_all[slot, first:last, :] = (swish * up).astype(BF16)
            gate_cot = (act_cot * up * sigma * (1.0 + gate * (1.0 - sigma))).astype(BF16)
            up_cot = (act_cot * swish).astype(BF16)
            cots_all[slot, first:last, 0:128] = gate_cot
            cots_all[slot, first:last, 128:256] = up_cot
            tin_all[first:last] += jnp.sum(
                gate_cot.astype(F32) * tail[:, 0:128] + up_cot.astype(F32) * tail[:, 128:256],
                axis=1,
                keepdims=True,
            )
            return carry

        lax.fori_loop(low, high, block, 0)

    def backward(first, last):
        def block(slot, carry):
            back[first:last] += dot_lanes(cots_all[slot, first:last], w_all[slot, :, 0:256])
            return carry

        back[first:last] = dot_lanes(cots_all[0, first:last], w_all[0, :, 0:256])
        lax.fori_loop(1, LINE, block, 0)
        for r in range(first, last, CAP):
            inverse = inv_all[r : r + CAP]
            unit = in_all[r : r + CAP].astype(F32) * inverse
            scaled = back[r : r + CAP] * gain_head
            inner = jnp.sum(scaled * unit, axis=1, keepdims=True) + tin_all[r : r + CAP] * inverse
            part_all[r : r + CAP] = (
                (scaled - unit * (inner / (2 * width))) * inverse
            ).astype(BF16)

    def part_of(step, lanes=slice(None)):
        row = Y_ROW[Y_ORDER.index(step)]
        return part_all.at[row : row + CAP, lanes]

    normalise(*NEAR)
    for copy in tail_copies + w_twin:
        copy.wait_recv()
    forward(*NEAR, 0, LINE - 1)
    ring[1, -1, 2].wait_recv()
    pass_on(1, -1, 3)
    ring[0, 1, 2].wait_recv()
    pass_on(0, 1, 3)
    first_twins = len(w_twin)
    w_far_a.wait_recv()
    swap(3, 0)
    w_far_b.wait_recv()
    swap(3, 1)
    normed_t[0] = normed[0 : FAR[0]].T
    cot_t[0] = cot_all[0 : FAR[0]].T
    for copy in w_twin[first_twins:]:
        copy.wait_recv()
    forward(*NEAR, LINE - 1, LINE)

    def near_product(slot, carry):
        g_acc[slot, :, 0:256] = dot(normed_t[0], cots_all[slot, 0 : FAR[0]])
        g_acc[slot, :, 256:384] = dot(cot_t[0], act_all[slot, 0 : FAR[0]])
        return carry

    lax.fori_loop(0, LINE, near_product, 0)
    backward(*NEAR)
    y_first = [
        send(part_of(1), y_in.at[0], y_dev(1)),
        send(part_of(-1), y_in.at[1], y_dev(-1)),
    ]

    ring[1, 1, 2].wait_recv()
    ring[0, -1, 2].wait_recv()
    ring[1, -1, 3].wait_recv()
    ring[0, 1, 3].wait_recv()
    normalise(*FAR)
    forward(*FAR, 0, LINE)
    normed_t[1] = normed[FAR[0] : ROWS].T
    cot_t[1] = cot_all[FAR[0] : ROWS].T

    def far_product(start, slot):
        wide = dot(normed_t[1, pl.ds(start, half)], cots_all[slot, FAR[0] : ROWS])
        narrow = dot(cot_t[1, pl.ds(start, half)], act_all[slot, FAR[0] : ROWS])
        return (
            wide + g_acc[slot, pl.ds(start, half), 0:256],
            narrow + g_acc[slot, pl.ds(start, half), 256:384],
        )

    their_start = pl.multiple_of((1 - core) * half, half)
    our_start = pl.multiple_of(core * half, half)

    def theirs(slot, carry):
        wide, narrow = far_product(their_start, slot)
        g_out[slot, :, 0:256] = wide.astype(BF16)
        g_out[slot, :, 256:384] = narrow.astype(BF16)
        return carry

    lax.fori_loop(0, LINE, theirs, 0)

    def cut(part):
        return slice(part * piece, (part + 1) * piece)

    pair_copies = [
        send(g_out.at[:, cut(part)], g_in.at[:, cut(part)], sibling) for part in range(PARTS)
    ]

    def ours(slot, carry):
        wide, narrow = far_product(our_start, slot)
        g_acc[slot, pl.ds(our_start, half), 0:256] = wide
        g_acc[slot, pl.ds(our_start, half), 256:384] = narrow
        return carry

    lax.fori_loop(0, LINE, ours, 0)

    x_first, x_second, z_first, z_second, z_near, z_far, last_copies = ({} for _ in range(7))

    def own_rows(part):
        return pl.ds(pl.multiple_of(core * half + part * piece, piece), piece)

    def x_start(part):
        pair_copies[part].wait_recv()

        def add(slot, carry):
            total = g_acc[slot, own_rows(part)] + g_in[slot, cut(part)].astype(F32)
            g_x[slot, cut(part)] = total.astype(BF16)
            return carry

        lax.fori_loop(1, LINE, add, 0)
        low = slice(part * piece, part * piece + mid)
        high = slice(part * piece + mid, (part + 1) * piece)
        x_first[part] = (
            send(g_x.at[3, low], x_opp.at[part, 0], x_dev(1)),
            send(g_x.at[3, high], x_opp.at[part, 1], x_dev(-1)),
            send(g_x.at[2, high], x_in.at[0, high], x_dev(1)),
            send(g_x.at[1, low], x_in.at[1, low], x_dev(-1)),
        )

    def x_relay(part):
        low = slice(part * piece, part * piece + mid)
        high = slice(part * piece + mid, (part + 1) * piece)
        x_first[part][0].wait_recv()
        g_x[2, low] = (g_x[2, low].astype(F32) + x_opp[part, 0].astype(F32)).astype(BF16)
        right = send(g_x.at[2, low], x_in.at[0, low], x_dev(1))
        x_first[part][1].wait_recv()
        g_x[1, high] = (g_x[1, high].astype(F32) + x_opp[part, 1].astype(F32)).astype(BF16)
        left = send(g_x.at[1, high], x_in.at[1, high], x_dev(-1))
        x_second[part] = (right, left)

    def z_cut(part, step):
        start = part * piece + lax.rem(z + step + n_z, n_z) * z_rows
        return pl.ds(pl.multiple_of(start, z_rows), z_rows)

    def z_start(part):
        for copy in x_first[part][2:] + x_second[part]:
            copy.wait_recv()
        h_all[cut(part)] = (
            g_acc[0, own_rows(part)]
            + g_in[0, cut(part)].astype(F32)
            + x_in[0, cut(part)].astype(F32)
            + x_in[1, cut(part)].astype(F32)
        ).astype(BF16)
        way = 1 if part % 2 == 0 else -1
        z_first[part] = (
            send(h_all.at[z_cut(part, 3)], z_relay.at[part, 0], z_dev(1)),
            send(h_all.at[z_cut(part, -3)], z_relay.at[part, 1], z_dev(-1)),
            send(h_all.at[z_cut(part, 4)], z_cross.at[part], z_dev(2 * way)),
            send(h_all.at[z_cut(part, 1)], z_in.at[part, 0], z_dev(1)),
            send(h_all.at[z_cut(part, -1)], z_in.at[part, 1], z_dev(-1)),
        )

    def z_join(part):
        for copy in z_first[part][:3]:
            copy.wait_recv()
        copies = []
        for side, step in ((0, 2), (1, -2)):
            total = h_all[z_cut(part, step)].astype(F32) + z_relay[part, side].astype(F32)
            if side == part % 2:
                total = total + z_cross[part].astype(F32)
            z_mid[part, side] = total.astype(BF16)
            copies.append(send(z_mid.at[part, side], z_in.at[part, 2 + side], z_dev(step)))
        z_second[part] = copies

    def z_final(part, step):
        start = core * half + part * piece + lax.rem(z + step + n_z, n_z) * z_rows
        return pl.ds(pl.multiple_of(start, z_rows), z_rows)

    def z_sum(part):
        for copy in z_first[part][3:] + tuple(z_second[part]):
            copy.wait_recv()
        total = h_all[z_cut(part, 0)].astype(F32)
        for index in range(4):
            total = total + z_in[part, index].astype(F32)
        final[z_final(part, 0)] = total.astype(BF16)
        mine = final.at[z_final(part, 0)]
        z_near[part] = [send(mine, mine, z_dev(step)) for step in (2, -2, 1, -1)]

    def z_spread(part):
        copies = []
        for side, step in ((0, 1), (1, -1)):
            z_near[part][side].wait_recv()
            theirs = final.at[z_final(part, -2 * step)]
            copies.append(send(theirs, theirs, z_dev(step)))
            if side == part % 2:
                copies.append(send(theirs, theirs, z_dev(2 * step)))
        z_far[part] = copies

    def z_end(part):
        for copy in z_near[part][2:] + z_far[part]:
            copy.wait_recv()
        mine = final.at[own_rows(part)]
        last_copies[part] = send(mine, mine, sibling)

    x_start(0)
    x_start(1)
    backward(*FAR)
    y_relays = [
        send(part_of(3), y_relay.at[0], y_dev(1)),
        send(part_of(-3), y_relay.at[1], y_dev(-1)),
        send(part_of(4, slice(0, half)), y_cross.at[0], y_dev(2)),
        send(part_of(4, slice(half, width)), y_cross.at[1], y_dev(-2)),
    ]
    x_relay(0)
    x_start(2)

    def tail_rows(slot, carry):
        row = jnp.sum(cots_all[slot].astype(F32) * inv_all[...], axis=0, keepdims=True)
        v_out[slot] = jnp.broadcast_to(row, (8, 256))
        return carry

    lax.fori_loop(0, LINE, tail_rows, 0)
    v_copies = [
        send(v_out.at[1], v_in.at[0], x_dev(-1)),
        send(v_out.at[2], v_in.at[1], x_dev(1)),
        send(v_out.at[3], v_in.at[2], x_dev(2)),
    ]

    z_start(0)
    x_relay(1)
    x_start(3)

    for copy in y_relays:
        copy.wait_recv()
    for side, step in ((0, 2), (1, -2)):
        row = Y_ROW[Y_ORDER.index(step)]
        total = part_all[row : row + CAP].astype(F32) + y_relay[side].astype(F32)
        cross = y_cross[side].astype(F32)
        lanes = slice(side * half, (side + 1) * half)
        other = slice((1 - side) * half, (2 - side) * half)
        y_mid[side, :, lanes] = (total[:, lanes] + cross).astype(BF16)
        y_mid[side, :, other] = total[:, other].astype(BF16)
        y_first.append(send(y_mid.at[side], y_in.at[2 + side], y_dev(step)))

    z_join(0)
    z_start(1)
    x_relay(2)

    for copy in v_copies:
        copy.wait_recv()
    v_pair[...] = v_out[0] + v_in[0] + v_in[1] + v_in[2]
    v_swap = send(v_pair, v_sib, sibling)

    z_sum(0)
    z_join(1)
    z_start(2)
    x_relay(3)

    v_swap.wait_recv()
    v_all[z] = v_pair[...] + v_sib[...]
    v_spread = [send(v_all.at[z], v_all.at[z], z_dev(step)) for step in range(1, n_z)]

    z_spread(0)
    z_sum(1)
    z_join(2)
    z_start(3)

    z_end(0)
    z_spread(1)
    z_sum(2)
    z_join(3)

    for copy in y_first:
        copy.wait_recv()
    widen_cot = part_all[0:CAP].astype(F32)
    for index in range(4):
        widen_cot = widen_cot + y_in[index].astype(F32)
    spread = dot_rows(chosen, cot_all[0:CAP]) + dot_rows(chosen, widen_cot.astype(BF16))
    ecot[...] = oc_ref[...].astype(F32) + spread
    for r in range(0, rows, CHUNK):
        g_mix[r : r + CHUNK] = ecot[r : r + CHUNK] * slope[r : r + CHUNK]
    edge_copy = send(g_mix.at[0:8], edge, before)

    z_end(1)
    z_spread(2)
    z_sum(3)

    z_end(2)
    z_spread(3)

    edge_copy.wait_recv()
    g_mix[rows : rows + 8] = edge[...] * (seq < n_seq - 1).astype(F32)
    for r in range(0, rows, CHUNK):
        grad = taps[0] * g_mix[r : r + CHUNK]
        for tap in range(1, KW):
            grad = grad + taps[tap] * g_mix[r + tap : r + tap + CHUNK]
        grad = grad * enc_gain
        value = x_ref[r : r + CHUNK].astype(F32)
        inverse = inv_x[r : r + CHUNK]
        inner = jnp.mean(grad * value, axis=1, keepdims=True) * (inverse * inverse)
        bg_ref[r : r + CHUNK] = (
            ecot[r : r + CHUNK] + (grad - value * inner) * inverse
        ).astype(BF16)

    for copy in v_spread:
        copy.wait_recv()
    v_total = v_all[0]
    for chip in range(1, n_z):
        v_total = v_total + v_all[chip]
    v_ref[...] = v_total

    z_end(3)
    for part in range(PARTS):
        last_copies[part].wait_recv()
    for copy in started:
        copy.wait_send()


def finish(
    bg, final, tail_b, v_ref, bg_out, gg_out, ug_out, dg_out, gg, ug, dg, sems
):
    width = final.shape[0]
    copies = []

    def store(source, target):
        copy = pltpu.make_async_copy(source, target, sems.at[len(copies)])
        copy.start()
        copies.append(copy)

    store(bg, bg_out)
    head, tail = slice(0, width), slice(width, 2 * width)
    gg[head] = final[:, 0:128].astype(F32)
    store(gg.at[head], gg_out.at[head])
    ug[head] = final[:, 128:256].astype(F32)
    store(ug.at[head], ug_out.at[head])
    gg[tail] = tail_b[...] * v_ref[0:1, 0:128]
    store(gg.at[tail], gg_out.at[tail])
    ug[tail] = tail_b[...] * v_ref[0:1, 128:256]
    store(ug.at[tail], ug_out.at[tail])
    dg[...] = final[:, 256:384].astype(F32).T
    store(dg, dg_out)
    for copy in copies:
        copy.wait()


def body(
    bytes_in,
    flags,
    enc_gain,
    conv_weight,
    widen,
    main_gain,
    gate_weight,
    up_weight,
    down_weight,
    out_cot,
):
    rows, width = bytes_in.shape[1:]
    n_y = lax.axis_size("seq") // LINE
    n_z = lax.axis_size("dp") // 2
    assert n_y == len(Y_ORDER)
    half = width // 2
    piece = half // PARTS
    z_rows = piece // n_z
    vmem = pl.BlockSpec(memory_space=pltpu.VMEM)
    hbm = pl.BlockSpec(memory_space=pltpu.HBM)
    scratch = [
        ((rows, width), BF16),
        ((1, rows), jnp.int32),
        ((8, width // 8), BF16),
        ((KW, width), BF16),
        ((8, width // 8), BF16),
        ((16, width // 8), BF16),
        ((width, 128), BF16),
        ((width, 128), BF16),
        ((128, width), BF16),
        ((rows, width), BF16),
        ((LINE, width, 384), BF16),
        ((LINE, 8, 256), F32),
        ((16, width), BF16),
        ((8, width), F32),
        ((8, width), F32),
        ((rows + 16, width), F32),
        ((rows, 1), F32),
        ((rows, width), BF16),
        ((rows, width), F32),
        ((ROWS, width), BF16),
        ((ROWS, width), BF16),
        ((ROWS, width), BF16),
        ((2, width, ROWS // 2), BF16),
        ((2, width, ROWS // 2), BF16),
        ((ROWS, 1), F32),
        ((ROWS, 1), F32),
        ((LINE, ROWS, 128), BF16),
        ((LINE, ROWS, 256), BF16),
        ((ROWS, width), F32),
        ((ROWS, width), BF16),
        ((4, CAP, width), BF16),
        ((2, CAP, width), BF16),
        ((2, CAP, half), BF16),
        ((2, CAP, width), BF16),
        ((LINE, 8, 256), F32),
        ((LINE - 1, 8, 256), F32),
        ((8, 256), F32),
        ((8, 256), F32),
        ((n_z, 8, 256), F32),
        ((LINE, width, 384), F32),
        ((LINE, half, 384), BF16),
        ((LINE, half, 384), BF16),
        ((LINE, half, 384), BF16),
        ((PARTS, 2, piece // 2, 384), BF16),
        ((2, half, 384), BF16),
        ((half, 384), BF16),
        ((PARTS, 4, z_rows, 384), BF16),
        ((PARTS, 2, z_rows, 384), BF16),
        ((PARTS, z_rows, 384), BF16),
        ((PARTS, 2, z_rows, 384), BF16),
        ((rows, width), F32),
        ((rows + 8, width), F32),
        ((8, width), F32),
    ]
    sums = pl.pallas_call(
        kernel,
        out_shape=(
            jax.ShapeDtypeStruct((rows, width), BF16),
            jax.ShapeDtypeStruct((width, 384), BF16),
            jax.ShapeDtypeStruct((width, 128), F32),
            jax.ShapeDtypeStruct((8, 256), F32),
        ),
        in_specs=[hbm] * 10,
        out_specs=[vmem] * 4,
        scratch_shapes=[pltpu.VMEM(shape, kind) for shape, kind in scratch]
        + [
            pltpu.SemaphoreType.DMA((12,)),
            pltpu.SemaphoreType.DMA((144,)),
            pltpu.SemaphoreType.DMA((144,)),
        ],
        compiler_params=pltpu.CompilerParams(
            collective_id=0, has_side_effects=True, vmem_limit_bytes=50 * 1024 * 1024
        ),
    )(
        bytes_in[0],
        flags,
        enc_gain.reshape(8, width // 8),
        conv_weight,
        widen.reshape(8, width // 8),
        main_gain.reshape(16, width // 8),
        gate_weight,
        up_weight,
        down_weight,
        out_cot[0],
    )
    outs = pl.pallas_call(
        finish,
        out_shape=(
            jax.ShapeDtypeStruct((rows, width), BF16),
            jax.ShapeDtypeStruct((2 * width, 128), F32),
            jax.ShapeDtypeStruct((2 * width, 128), F32),
            jax.ShapeDtypeStruct((128, width), F32),
        ),
        in_specs=[vmem] * 4,
        out_specs=[hbm] * 4,
        scratch_shapes=[
            pltpu.VMEM((2 * width, 128), F32),
            pltpu.VMEM((2 * width, 128), F32),
            pltpu.VMEM((128, width), F32),
            pltpu.SemaphoreType.DMA((6,)),
        ],
        compiler_params=pltpu.CompilerParams(vmem_limit_bytes=8 * 1024 * 1024),
    )(*sums)
    return (outs[0][None], outs[1], outs[2], outs[3])


def solution(mesh):
    in_specs = (
        P("dp", "seq", None),
        P("dp", "seq"),
        P(),
        P(),
        P(),
        P(),
        P(None, "seq"),
        P(None, "seq"),
        P("seq", None),
        P("dp", "seq", None),
    )
    out_specs = (P("dp", "seq", None), P(None, "seq"), P(None, "seq"), P("seq", None))
    return jax.shard_map(body, mesh=mesh, in_specs=in_specs, out_specs=out_specs, check_vma=False)
```

time: 91.4 us -> 96.6 us (1.057); the launches traced: 90 us -> 96.2 us
  Pallas kernels: 78.2 us -> 87.8 us
  local copies, waits for them, and re-layouts: 11 us -> 7.66 us
    pallas_call x1, Pallas kernels: 78.2 us -> 86.2 us  [body(): pl.pallas_call(kernel, out_shape=(jax.ShapeDtypeStruct((rows, width), BF1...]
    unnamed x24 -> x20, local copies, waits for them, and re-layouts: 11 us -> 7.66 us
    pallas_call x0 -> x1, Pallas kernels: none -> 1.64 us  [body(): pl.pallas_call(finish, out_shape=(jax.ShapeDtypeStruct((rows, width), BF1...]
where the time goes in v2:
time: 96.6 us; the launch traced here: 96.2 us
  Pallas kernels  87.8 us (91%)
  local copies, waits for them, and re-layouts  7.66 us (8%)
    pallas_call x1, Pallas kernels, body(): pl.pallas_call(kernel, out_shape=(jax.ShapeDtypeStruct((rows, width), BF1...  86.2 us
    unnamed x20, local copies, waits for them, and re-layouts  7.66 us

profile of v2, /device:TPU:1, one launch (start us, length us, event | category | flops | bytes accessed | tf_op | source)
XLA Modules:
  0.0 96.2 jit_solution(17777451650872769889)
XLA Ops:
  0.6 0.0 copy-start.5
  0.6 0.0 copy-start.9
  0.7 0.7 copy-done.5
  1.3 0.0 copy-done.9
  1.3 0.0 copy-start
  1.3 1.0 %copy-done = bf16[2048,128]{1,0:T(8,128)(2,1)S(1)} copy-done((bf16[2048,128]{1,0:T(8,128)(2,1)S(1)}, bf16[2048,128]{1,0:T(8,128)(2,1)}, u32[]{:S(2)}) %copy-start) | copy-done | bytes 524312
  2.4 0.0 copy-start.1
  2.4 1.0 %copy-done.1 = bf16[2048,128]{1,0:T(8,128)(2,1)S(1)} copy-done((bf16[2048,128]{1,0:T(8,128)(2,1)S(1)}, bf16[2048,128]{1,0:T(8,128)(2,1)}, u32[]{:S(2)}) %copy-start.1) | copy-done | bytes 524312
  3.4 0.0 copy-start.2
  3.4 0.9 copy-done.2
  4.4 0.0 copy-start.3
  4.4 0.9 copy-done.3
  5.3 0.0 copy-start.4
  5.3 0.9 copy-done.4
  6.3 0.0 copy-start.6
  6.3 0.7 copy-done.6
  7.0 0.0 copy-start.7
  7.0 0.7 copy-done.7
  7.6 0.0 copy-start.8
  7.6 0.7 copy-done.8
  8.3 86.2 %shard_map.129 = (bf16[128,1024]{1,0:T(8,128)(2,1)S(1)}, bf16[1024,384]{1,0:T(8,128)(2,1)S(1)}, f32[1024,128]{1,0:T(8,128)S(1)}, f32[8,256]{1,0:T(8,128)S(1)}) custom-call(bf16[128,1024]{1,0:T(8,128)(2,1)S(1)} %bitcast.6, s32[1,128]{1,0:T(1,128)S(1)} %copy-done.9, bf16[8,128]{1,0:T(8,128)(2,1)S(1)} %bitcast.9, bf16[4,1024]{1,0:T(4,128)(2,1)S(1)} %copy-done.5, ...), custom_call_target="tpu_custom_call" | custom-call | tf_op jit(solution)/shard_map/pallas_call | solution.py:757
  94.5 1.6 %shard_map.130 = (bf16[128,1024]{1,0:T(8,128)(2,1)}, f32[2048,128]{1,0:T(8,128)}, f32[2048,128]{1,0:T(8,128)}, f32[128,1024]{1,0:T(8,128)}) custom-call(bf16[128,1024]{1,0:T(8,128)(2,1)S(1)} %get-tuple-element.12.bg, bf16[1024,384]{1,0:T(8,128)(2,1)S(1)} %get-tuple-element.13.final, f32[1024,128]{1,0:T(8,128)S(1)} %get-tuple-element.14.tail_b, ...), custom_call_target="tpu_custom_call" | custom-call | tf_op jit(solution)/shard_map/pallas_call | solution.py:788
Async XLA Ops:
  0.6 0.7 copy-start.5
  0.6 0.7 copy-start.9
  1.3 1.0 %copy-start = (bf16[2048,128]{1,0:T(8,128)(2,1)S(1)}, bf16[2048,128]{1,0:T(8,128)(2,1)}, u32[]{:S(2)}) copy-start(bf16[2048,128]{1,0:T(8,128)(2,1)} %gw_hbm.1) | copy-start | bytes 1572868
  2.4 1.0 %copy-start.1 = (bf16[2048,128]{1,0:T(8,128)(2,1)S(1)}, bf16[2048,128]{1,0:T(8,128)(2,1)}, u32[]{:S(2)}) copy-start(bf16[2048,128]{1,0:T(8,128)(2,1)} %uw_hbm.1) | copy-start | bytes 1572868
  3.4 0.9 copy-start.2
  4.4 0.9 copy-start.3
  5.3 0.9 copy-start.4
  6.3 0.7 copy-start.6
  7.0 0.7 copy-start.7
  7.6 0.7 copy-start.8

commit v3 on v2

--- a/solution.py
+++ b/solution.py
@@ -13,7 +13,8 @@
 CAP = 48
 EPS = 1e-05
 LINE = 4
-PARTS = 4
+PIECES = (0, 256, 384, 512)
+PARTS = len(PIECES) - 1
 CHUNK = 32
 
 Y_ORDER = (0, -1, 1, -2, 2, -3, 3, 4)
@@ -52,6 +53,10 @@
     uw_hbm,
     dw_hbm,
     oc_hbm,
+    bg_hbm,
+    final_hbm,
+    tail_hbm,
+    v_hbm,
     bg_ref,
     final,
     tail_b,
@@ -87,9 +92,6 @@
     back,
     part_all,
     y_in,
-    y_relay,
-    y_cross,
-    y_mid,
     v_out,
     v_in,
     v_pair,
@@ -103,13 +105,11 @@
     x_in,
     h_all,
     z_in,
-    z_relay,
-    z_cross,
-    z_mid,
     ecot,
     g_mix,
     edge,
     load_sems,
+    store_sems,
     send_sems,
     recv_sems,
 ):
@@ -122,9 +122,6 @@
     y, x = seq // LINE, seq % LINE
     rows, width = x_ref.shape
     half = width // 2
-    piece = half // PARTS
-    mid = piece // 2
-    z_rows = piece // n_z
 
     def y_dev(step):
         return {"seq": lax.rem(y + step + n_y, n_y) * LINE + x}
@@ -140,6 +137,7 @@
     before = {"seq": lax.rem(seq + n_seq - 1, n_seq)}
 
     loads = []
+    stores = []
 
     def load(source, target):
         copy = pltpu.make_async_copy(source, target, load_sems.at[len(loads)])
@@ -147,8 +145,38 @@
         loads.append(copy)
         return copy
 
+    def store(source, target):
+        copy = pltpu.make_async_copy(source, target, store_sems.at[len(stores)])
+        copy.start()
+        stores.append(copy)
+
     load_marks = load(marks_hbm, marks_ref)
     load_oc = load(oc_hbm, oc_ref)
+
+    started = []
+
+    def send(source, target, device):
+        index = len(started)
+        copy = pltpu.make_async_remote_copy(
+            src_ref=source,
+            dst_ref=target,
+            send_sem=send_sems.at[index],
+            recv_sem=recv_sems.at[index],
+            device_id=device,
+            device_id_type=MESH,
+        )
+        copy.start()
+        started.append(copy)
+        return copy
+
+    barrier = pltpu.get_barrier_semaphore()
+    peers = [y_dev(step) for step in range(1, n_y)]
+    peers += [x_dev(step) for step in (1, -1, 2)]
+    peers += [z_dev(step) for step in range(1, n_z)]
+    peers += [sibling, after, before]
+    for peer in peers:
+        pl.semaphore_signal(barrier, inc=1, device_id=peer, device_id_type=MESH)
+
     load_x = load(x_hbm, x_ref)
     load_gain = load(enc_gain_hbm, enc_gain_ref)
     load_conv = load(conv_hbm, conv_ref)
@@ -163,30 +191,6 @@
         load(gw_hbm.at[width : 2 * width], gw_tail),
         load(uw_hbm.at[width : 2 * width], uw_tail),
     ]
-
-    started = []
-
-    def send(source, target, device):
-        index = len(started)
-        copy = pltpu.make_async_remote_copy(
-            src_ref=source,
-            dst_ref=target,
-            send_sem=send_sems.at[index],
-            recv_sem=recv_sems.at[index],
-            device_id=device,
-            device_id_type=MESH,
-        )
-        copy.start()
-        started.append(copy)
-        return copy
-
-    barrier = pltpu.get_barrier_semaphore()
-    peers = [y_dev(step) for step in (1, -1, 2, -2)]
-    peers += [x_dev(step) for step in (1, -1, 2)]
-    peers += [z_dev(step) for step in range(1, n_z)]
-    peers += [sibling, after, before]
-    for peer in peers:
-        pl.semaphore_signal(barrier, inc=1, device_id=peer, device_id_type=MESH)
 
     load_marks.wait()
     marks = marks_ref[...].astype(F32)
@@ -284,6 +288,7 @@
     tail_vec = widen * main_gain[:, width : 2 * width]
     tail_square = jnp.sum(widen * widen, axis=1, keepdims=True)
     tail_b[...] = jnp.broadcast_to(tail_vec, (128, width)).T
+    store(tail_b, tail_hbm)
     tail_gate = jnp.sum(gw_tail[...].astype(F32) * tail_b[...], axis=0, keepdims=True)
     tail_up = jnp.sum(uw_tail[...].astype(F32) * tail_b[...], axis=0, keepdims=True)
     tails[0, :, 0:128] = jnp.broadcast_to(tail_gate, (8, 128))
@@ -361,9 +366,12 @@
                 (scaled - unit * (inner / (2 * width))) * inverse
             ).astype(BF16)
 
-    def part_of(step, lanes=slice(None)):
+    y_copies = []
+
+    def y_send(step):
         row = Y_ROW[Y_ORDER.index(step)]
-        return part_all.at[row : row + CAP, lanes]
+        there = Y_ORDER.index(4 if step == 4 else -step)
+        y_copies.append(send(part_all.at[row : row + CAP], y_in.at[there], y_dev(step)))
 
     normalise(*NEAR)
     for copy in tail_copies + w_twin:
@@ -391,10 +399,8 @@
 
     lax.fori_loop(0, LINE, near_product, 0)
     backward(*NEAR)
-    y_first = [
-        send(part_of(1), y_in.at[0], y_dev(1)),
-        send(part_of(-1), y_in.at[1], y_dev(-1)),
-    ]
+    for step in (2, -2, 1, -1):
+        y_send(step)
 
     ring[1, 1, 2].wait_recv()
     ring[0, -1, 2].wait_recv()
@@ -425,7 +431,12 @@
     lax.fori_loop(0, LINE, theirs, 0)
 
     def cut(part):
-        return slice(part * piece, (part + 1) * piece)
+        return slice(PIECES[part], PIECES[part + 1])
+
+    def halves(part):
+        first, last = PIECES[part], PIECES[part + 1]
+        mid = (first + last) // 2
+        return slice(first, mid), slice(mid, last)
 
     pair_copies = [
         send(g_out.at[:, cut(part)], g_in.at[:, cut(part)], sibling) for part in range(PARTS)
@@ -439,10 +450,14 @@
 
     lax.fori_loop(0, LINE, ours, 0)
 
-    x_first, x_second, z_first, z_second, z_near, z_far, last_copies = ({} for _ in range(7))
+    x_first, x_second, z_first, z_near, z_far, last_copies = ({} for _ in range(6))
+
+    def rows_of(which, part):
+        count = PIECES[part + 1] - PIECES[part]
+        return pl.ds(pl.multiple_of(which * half + PIECES[part], 128), count)
 
     def own_rows(part):
-        return pl.ds(pl.multiple_of(core * half + part * piece, piece), piece)
+        return rows_of(core, part)
 
     def x_start(part):
         pair_copies[part].wait_recv()
@@ -453,29 +468,31 @@
             return carry
 
         lax.fori_loop(1, LINE, add, 0)
-        low = slice(part * piece, part * piece + mid)
-        high = slice(part * piece + mid, (part + 1) * piece)
+        low, high = halves(part)
         x_first[part] = (
-            send(g_x.at[3, low], x_opp.at[part, 0], x_dev(1)),
-            send(g_x.at[3, high], x_opp.at[part, 1], x_dev(-1)),
+            send(g_x.at[3, low], x_opp.at[low], x_dev(1)),
+            send(g_x.at[3, high], x_opp.at[high], x_dev(-1)),
             send(g_x.at[2, high], x_in.at[0, high], x_dev(1)),
             send(g_x.at[1, low], x_in.at[1, low], x_dev(-1)),
         )
 
     def x_relay(part):
-        low = slice(part * piece, part * piece + mid)
-        high = slice(part * piece + mid, (part + 1) * piece)
+        low, high = halves(part)
         x_first[part][0].wait_recv()
-        g_x[2, low] = (g_x[2, low].astype(F32) + x_opp[part, 0].astype(F32)).astype(BF16)
+        g_x[2, low] = (g_x[2, low].astype(F32) + x_opp[low].astype(F32)).astype(BF16)
         right = send(g_x.at[2, low], x_in.at[0, low], x_dev(1))
         x_first[part][1].wait_recv()
-        g_x[1, high] = (g_x[1, high].astype(F32) + x_opp[part, 1].astype(F32)).astype(BF16)
+        g_x[1, high] = (g_x[1, high].astype(F32) + x_opp[high].astype(F32)).astype(BF16)
         left = send(g_x.at[1, high], x_in.at[1, high], x_dev(-1))
         x_second[part] = (right, left)
 
-    def z_cut(part, step):
-        start = part * piece + lax.rem(z + step + n_z, n_z) * z_rows
-        return pl.ds(pl.multiple_of(start, z_rows), z_rows)
+    def z_cut(part, step, base=0):
+        count = (PIECES[part + 1] - PIECES[part]) // n_z
+        start = base + PIECES[part] + lax.rem(z + step + n_z, n_z) * count
+        return pl.ds(pl.multiple_of(start, 16), count)
+
+    def z_slot(part):
+        return slice(PIECES[part] // n_z, PIECES[part + 1] // n_z)
 
     def z_start(part):
         for copy in x_first[part][2:] + x_second[part]:
@@ -486,37 +503,19 @@
             + x_in[0, cut(part)].astype(F32)
             + x_in[1, cut(part)].astype(F32)
         ).astype(BF16)
-        way = 1 if part % 2 == 0 else -1
-        z_first[part] = (
-            send(h_all.at[z_cut(part, 3)], z_relay.at[part, 0], z_dev(1)),
-            send(h_all.at[z_cut(part, -3)], z_relay.at[part, 1], z_dev(-1)),
-            send(h_all.at[z_cut(part, 4)], z_cross.at[part], z_dev(2 * way)),
-            send(h_all.at[z_cut(part, 1)], z_in.at[part, 0], z_dev(1)),
-            send(h_all.at[z_cut(part, -1)], z_in.at[part, 1], z_dev(-1)),
-        )
-
-    def z_join(part):
-        for copy in z_first[part][:3]:
+        z_first[part] = [
+            send(h_all.at[z_cut(part, step)], z_in.at[index, z_slot(part)], z_dev(step))
+            for index, step in enumerate((4, 3, -3, 2, -2, 1, -1))
+        ]
+
+    def z_final(part, step):
+        return z_cut(part, step, core * half)
+
+    def z_sum(part):
+        total = h_all[z_cut(part, 0)].astype(F32)
+        for index, copy in enumerate(z_first[part]):
             copy.wait_recv()
-        copies = []
-        for side, step in ((0, 2), (1, -2)):
-            total = h_all[z_cut(part, step)].astype(F32) + z_relay[part, side].astype(F32)
-            if side == part % 2:
-                total = total + z_cross[part].astype(F32)
-            z_mid[part, side] = total.astype(BF16)
-            copies.append(send(z_mid.at[part, side], z_in.at[part, 2 + side], z_dev(step)))
-        z_second[part] = copies
-
-    def z_final(part, step):
-        start = core * half + part * piece + lax.rem(z + step + n_z, n_z) * z_rows
-        return pl.ds(pl.multiple_of(start, z_rows), z_rows)
-
-    def z_sum(part):
-        for copy in z_first[part][3:] + tuple(z_second[part]):
-            copy.wait_recv()
-        total = h_all[z_cut(part, 0)].astype(F32)
-        for index in range(4):
-            total = total + z_in[part, index].astype(F32)
+            total = total + z_in[index, z_slot(part)].astype(F32)
         final[z_final(part, 0)] = total.astype(BF16)
         mine = final.at[z_final(part, 0)]
         z_near[part] = [send(mine, mine, z_dev(step)) for step in (2, -2, 1, -1)]
@@ -527,7 +526,7 @@
             z_near[part][side].wait_recv()
             theirs = final.at[z_final(part, -2 * step)]
             copies.append(send(theirs, theirs, z_dev(step)))
-            if side == part % 2:
+            if side == min(part, 1):
                 copies.append(send(theirs, theirs, z_dev(2 * step)))
         z_far[part] = copies
 
@@ -540,14 +539,11 @@
     x_start(0)
     x_start(1)
     backward(*FAR)
-    y_relays = [
-        send(part_of(3), y_relay.at[0], y_dev(1)),
-        send(part_of(-3), y_relay.at[1], y_dev(-1)),
-        send(part_of(4, slice(0, half)), y_cross.at[0], y_dev(2)),
-        send(part_of(4, slice(half, width)), y_cross.at[1], y_dev(-2)),
-    ]
+    for step in (4, 3, -3):
+        y_send(step)
     x_relay(0)
     x_start(2)
+    x_relay(1)
 
     def tail_rows(slot, carry):
         row = jnp.sum(cots_all[slot].astype(F32) * inv_all[...], axis=0, keepdims=True)
@@ -560,55 +556,30 @@
         send(v_out.at[2], v_in.at[1], x_dev(1)),
         send(v_out.at[3], v_in.at[2], x_dev(2)),
     ]
-
+    x_relay(2)
     z_start(0)
-    x_relay(1)
-    x_start(3)
-
-    for copy in y_relays:
-        copy.wait_recv()
-    for side, step in ((0, 2), (1, -2)):
-        row = Y_ROW[Y_ORDER.index(step)]
-        total = part_all[row : row + CAP].astype(F32) + y_relay[side].astype(F32)
-        cross = y_cross[side].astype(F32)
-        lanes = slice(side * half, (side + 1) * half)
-        other = slice((1 - side) * half, (2 - side) * half)
-        y_mid[side, :, lanes] = (total[:, lanes] + cross).astype(BF16)
-        y_mid[side, :, other] = total[:, other].astype(BF16)
-        y_first.append(send(y_mid.at[side], y_in.at[2 + side], y_dev(step)))
-
-    z_join(0)
-    z_start(1)
-    x_relay(2)
 
     for copy in v_copies:
         copy.wait_recv()
     v_pair[...] = v_out[0] + v_in[0] + v_in[1] + v_in[2]
     v_swap = send(v_pair, v_sib, sibling)
 
-    z_sum(0)
-    z_join(1)
-    z_start(2)
-    x_relay(3)
-
+    z_start(1)
     v_swap.wait_recv()
     v_all[z] = v_pair[...] + v_sib[...]
     v_spread = [send(v_all.at[z], v_all.at[z], z_dev(step)) for step in range(1, n_z)]
-
+    z_sum(0)
+    z_start(2)
+    z_sum(1)
     z_spread(0)
-    z_sum(1)
-    z_join(2)
-    z_start(3)
-
-    z_end(0)
+    z_sum(2)
     z_spread(1)
-    z_sum(2)
-    z_join(3)
-
-    for copy in y_first:
+    early = len(started)
+
+    for copy in y_copies:
         copy.wait_recv()
     widen_cot = part_all[0:CAP].astype(F32)
-    for index in range(4):
+    for index in range(1, n_y):
         widen_cot = widen_cot + y_in[index].astype(F32)
     spread = dot_rows(chosen, cot_all[0:CAP]) + dot_rows(chosen, widen_cot.astype(BF16))
     ecot[...] = oc_ref[...].astype(F32) + spread
@@ -616,12 +587,8 @@
         g_mix[r : r + CHUNK] = ecot[r : r + CHUNK] * slope[r : r + CHUNK]
     edge_copy = send(g_mix.at[0:8], edge, before)
 
-    z_end(1)
     z_spread(2)
-    z_sum(3)
-
-    z_end(2)
-    z_spread(3)
+    z_end(0)
 
     edge_copy.wait_recv()
     g_mix[rows : rows + 8] = edge[...] * (seq < n_seq - 1).astype(F32)
@@ -636,6 +603,7 @@
         bg_ref[r : r + CHUNK] = (
             ecot[r : r + CHUNK] + (grad - value * inner) * inverse
         ).astype(BF16)
+    store(bg_ref, bg_hbm)
 
     for copy in v_spread:
         copy.wait_recv()
@@ -643,39 +611,57 @@
     for chip in range(1, n_z):
         v_total = v_total + v_all[chip]
     v_ref[...] = v_total
-
-    z_end(3)
+    store(v_ref, v_hbm)
+
+    z_end(1)
+    for copy in started[:early]:
+        copy.wait_send()
+    z_end(2)
+    for part in range(PARTS):
+        store(final.at[own_rows(part)], final_hbm.at[own_rows(part)])
     for part in range(PARTS):
         last_copies[part].wait_recv()
-    for copy in started:
+        store(final.at[rows_of(1 - core, part)], final_hbm.at[rows_of(1 - core, part)])
+    for copy in started[early:]:
         copy.wait_send()
+    for copy in stores:
+        copy.wait()
 
 
 def finish(
-    bg, final, tail_b, v_ref, bg_out, gg_out, ug_out, dg_out, gg, ug, dg, sems
+    bg_hbm, final_hbm, tail_hbm, v_hbm, bg_out, gg_out, ug_out, dg_out, bg, final, tail_b, v_ref, gg, ug, dg, sems
 ):
     width = final.shape[0]
     copies = []
 
-    def store(source, target):
-        copy = pltpu.make_async_copy(source, target, sems.at[len(copies)])
-        copy.start()
-        copies.append(copy)
-
-    store(bg, bg_out)
+    def copy(source, target):
+        step = pltpu.make_async_copy(source, target, sems.at[len(copies)])
+        step.start()
+        copies.append(step)
+        return step
+
+    load_final = copy(final_hbm, final)
+    load_tail = copy(tail_hbm, tail_b)
+    load_v = copy(v_hbm, v_ref)
+    load_bg = copy(bg_hbm, bg)
     head, tail = slice(0, width), slice(width, 2 * width)
+    load_final.wait()
     gg[head] = final[:, 0:128].astype(F32)
-    store(gg.at[head], gg_out.at[head])
+    copy(gg.at[head], gg_out.at[head])
     ug[head] = final[:, 128:256].astype(F32)
-    store(ug.at[head], ug_out.at[head])
+    copy(ug.at[head], ug_out.at[head])
+    load_bg.wait()
+    copy(bg, bg_out)
+    load_tail.wait()
+    load_v.wait()
     gg[tail] = tail_b[...] * v_ref[0:1, 0:128]
-    store(gg.at[tail], gg_out.at[tail])
+    copy(gg.at[tail], gg_out.at[tail])
     ug[tail] = tail_b[...] * v_ref[0:1, 128:256]
-    store(ug.at[tail], ug_out.at[tail])
+    copy(ug.at[tail], ug_out.at[tail])
     dg[...] = final[:, 256:384].astype(F32).T
-    store(dg, dg_out)
-    for copy in copies:
-        copy.wait()
+    copy(dg, dg_out)
+    for step in copies[4:]:
+        step.wait()
 
 
 def body(
@@ -695,11 +681,12 @@
     n_z = lax.axis_size("dp") // 2
     assert n_y == len(Y_ORDER)
     half = width // 2
-    piece = half // PARTS
-    z_rows = piece // n_z
-    vmem = pl.BlockSpec(memory_space=pltpu.VMEM)
     hbm = pl.BlockSpec(memory_space=pltpu.HBM)
     scratch = [
+        ((rows, width), BF16),
+        ((width, 384), BF16),
+        ((width, 128), F32),
+        ((8, 256), F32),
         ((rows, width), BF16),
         ((1, rows), jnp.int32),
         ((8, width // 8), BF16),
@@ -730,10 +717,7 @@
         ((LINE, ROWS, 256), BF16),
         ((ROWS, width), F32),
         ((ROWS, width), BF16),
-        ((4, CAP, width), BF16),
-        ((2, CAP, width), BF16),
-        ((2, CAP, half), BF16),
-        ((2, CAP, width), BF16),
+        ((n_y, CAP, width), BF16),
         ((LINE, 8, 256), F32),
         ((LINE - 1, 8, 256), F32),
         ((8, 256), F32),
@@ -743,13 +727,10 @@
         ((LINE, half, 384), BF16),
         ((LINE, half, 384), BF16),
         ((LINE, half, 384), BF16),
-        ((PARTS, 2, piece // 2, 384), BF16),
+        ((half, 384), BF16),
         ((2, half, 384), BF16),
         ((half, 384), BF16),
-        ((PARTS, 4, z_rows, 384), BF16),
-        ((PARTS, 2, z_rows, 384), BF16),
-        ((PARTS, z_rows, 384), BF16),
-        ((PARTS, 2, z_rows, 384), BF16),
+        ((n_z - 1, half // n_z, 384), BF16),
         ((rows, width), F32),
         ((rows + 8, width), F32),
         ((8, width), F32),
@@ -763,15 +744,16 @@
             jax.ShapeDtypeStruct((8, 256), F32),
         ),
         in_specs=[hbm] * 10,
-        out_specs=[vmem] * 4,
+        out_specs=[hbm] * 4,
         scratch_shapes=[pltpu.VMEM(shape, kind) for shape, kind in scratch]
         + [
             pltpu.SemaphoreType.DMA((12,)),
-            pltpu.SemaphoreType.DMA((144,)),
-            pltpu.SemaphoreType.DMA((144,)),
+            pltpu.SemaphoreType.DMA((9,)),
+            pltpu.SemaphoreType.DMA((120,)),
+            pltpu.SemaphoreType.DMA((120,)),
         ],
         compiler_params=pltpu.CompilerParams(
-            collective_id=0, has_side_effects=True, vmem_limit_bytes=50 * 1024 * 1024
+            collective_id=0, has_side_effects=True, vmem_limit_bytes=60 * 1024 * 1024
         ),
     )(
         bytes_in[0],
@@ -793,15 +775,19 @@
             jax.ShapeDtypeStruct((2 * width, 128), F32),
             jax.ShapeDtypeStruct((128, width), F32),
         ),
-        in_specs=[vmem] * 4,
+        in_specs=[hbm] * 4,
         out_specs=[hbm] * 4,
         scratch_shapes=[
+            pltpu.VMEM((rows, width), BF16),
+            pltpu.VMEM((width, 384), BF16),
+            pltpu.VMEM((width, 128), F32),
+            pltpu.VMEM((8, 256), F32),
             pltpu.VMEM((2 * width, 128), F32),
             pltpu.VMEM((2 * width, 128), F32),
             pltpu.VMEM((128, width), F32),
-            pltpu.SemaphoreType.DMA((6,)),
+            pltpu.SemaphoreType.DMA((10,)),
         ],
-        compiler_params=pltpu.CompilerParams(vmem_limit_bytes=8 * 1024 * 1024),
+        compiler_params=pltpu.CompilerParams(vmem_limit_bytes=60 * 1024 * 1024),
     )(*sums)
     return (outs[0][None], outs[1], outs[2], outs[3])
 

time: 96.6 us -> 85.4 us (0.88)
  local copies, waits for them, and re-layouts: 7.66 us -> 0 us
  Pallas kernels: 87.8 us -> 84.6 us
    unnamed x20 -> x0, local copies, waits for them, and re-layouts: 7.66 us -> none
    pallas_call x1, Pallas kernels: 86.2 us -> 81.7 us  [body(): pl.pallas_call(kernel, out_shape=(jax.ShapeDtypeStruct((rows, width), BF1...]
    pallas_call x1, Pallas kernels: 1.64 us -> 2.82 us  [body(): pl.pallas_call(finish, out_shape=(jax.ShapeDtypeStruct((rows, width), BF1...]
where the time goes in v3:
time: 85.4 us; the launch traced here: 85.2 us
  Pallas kernels  84.6 us (99%)
    pallas_call x1, Pallas kernels, body(): pl.pallas_call(kernel, out_shape=(jax.ShapeDtypeStruct((rows, width), BF1...  81.7 us
    pallas_call x1, Pallas kernels, body(): pl.pallas_call(finish, out_shape=(jax.ShapeDtypeStruct((rows, width), BF1...  2.82 us

profile of v3, /device:TPU:1, one launch (start us, length us, event | category | flops | bytes accessed | tf_op | source)
XLA Modules:
  0.0 85.2 jit_solution(6886402860056842871)
XLA Ops:
  0.6 81.7 %shard_map.129 = (bf16[128,1024]{1,0:T(8,128)(2,1)}, bf16[1024,384]{1,0:T(8,128)(2,1)}, f32[1024,128]{1,0:T(8,128)}, f32[8,256]{1,0:T(8,128)}) custom-call(bf16[128,1024]{1,0:T(8,128)(2,1)} %bitcast.6, s32[1,128]{1,0:T(1,128)} %marks_hbm.1, bf16[8,128]{1,0:T(8,128)(2,1)} %bitcast.9, bf16[4,1024]{1,0:T(4,128)(2,1)} %conv_hbm.1, bf16[8,128]{1,0:T(8,128)(2,1)} %bitcast.10, ...), custom_call_target="tpu_custom_call" | custom-call | tf_op jit(solution)/shard_map/pallas_call | solution.py:738
  82.4 2.8 %shard_map.130 = (bf16[128,1024]{1,0:T(8,128)(2,1)}, f32[2048,128]{1,0:T(8,128)}, f32[2048,128]{1,0:T(8,128)}, f32[128,1024]{1,0:T(8,128)}) custom-call(bf16[128,1024]{1,0:T(8,128)(2,1)} %get-tuple-element.12.bg_hbm, bf16[1024,384]{1,0:T(8,128)(2,1)} %get-tuple-element.13.final_hbm, f32[1024,128]{1,0:T(8,128)} %get-tuple-element.14.tail_hbm, ...), custom_call_target="tpu_custom_call" | custom-call | tf_op jit(solution)/shard_map/pallas_call | solution.py:770

commit v4 on v3

--- a/solution.py
+++ b/solution.py
@@ -13,7 +13,7 @@
 CAP = 48
 EPS = 1e-05
 LINE = 4
-PIECES = (0, 256, 384, 512)
+PIECES = (0, 128, 384, 512)
 PARTS = len(PIECES) - 1
 CHUNK = 32
 
@@ -232,7 +232,7 @@
     def pass_on(which, direction, step):
         buffer = (in_all, cot_all)[which]
         here = Y_ROW[Y_ORDER.index(-direction * step)]
-        there = Y_ROW[Y_ORDER.index(4 if step == 3 else -direction * (step + 1))]
+        there = Y_ROW[Y_ORDER.index(-direction * (step + 1))]
         ring[which, direction, step] = send(
             buffer.at[here : here + CAP], buffer.at[there : there + CAP], y_dev(direction)
         )
@@ -273,13 +273,6 @@
     def swap(slot, part):
         w_twin.append(send(w_rows(slot, part), w_rows(slot, part), sibling))
 
-    w_right[0].wait_recv()
-    w_far_a = send(w_rows(1, 0), w_rows(3, 0), x_dev(1))
-    w_left[1].wait_recv()
-    w_far_b = send(w_rows(2, 1), w_rows(3, 1), x_dev(-1))
-    swap(1, 0)
-    swap(2, 1)
-
     for copy in load_tail:
         copy.wait()
     widen = as_row(widen_ref[...])
@@ -299,17 +292,32 @@
         send(tails.at[0], tails.at[3], x_dev(2)),
     ]
 
-    def relay(step):
-        for which in (1, 0):
-            for direction in (1, -1):
-                ring[which, direction, step - 1].wait_recv()
-                pass_on(which, direction, step)
-
-    relay(1)
-    w_right[1].wait_recv()
-    swap(1, 1)
-    w_left[0].wait_recv()
-    swap(2, 0)
+    def relay(which, step):
+        for direction in (1, -1):
+            ring[which, direction, step - 1].wait_recv()
+            pass_on(which, direction, step)
+
+    def relay_last(which):
+        buffer = (in_all, cot_all)[which]
+        there = Y_ROW[Y_ORDER.index(4)]
+        for direction in (1, -1):
+            ring[which, direction, 2].wait_recv()
+            here = Y_ROW[Y_ORDER.index(-3 * direction)]
+            lanes = slice(0, half) if direction == 1 else slice(half, width)
+            ring[which, direction, 3] = send(
+                buffer.at[here : here + CAP, lanes],
+                buffer.at[there : there + CAP, lanes],
+                y_dev(direction),
+            )
+
+    relay(1, 1)
+    relay(0, 1)
+    w_right[0].wait_recv()
+    w_far_a = send(w_rows(1, 0), w_rows(3, 0), x_dev(1))
+    w_left[1].wait_recv()
+    w_far_b = send(w_rows(2, 1), w_rows(3, 1), x_dev(-1))
+    swap(1, 0)
+    swap(2, 1)
     for first, last in ((NEAR[1], FAR[0]), (FAR[1], ROWS)):
         count = last - first
         normed[first:last] = jnp.zeros((count, width), BF16)
@@ -317,7 +325,12 @@
         inv_all[first:last] = jnp.zeros((count, 1), F32)
         act_all[:, first:last] = jnp.zeros((LINE, count, 128), BF16)
         cots_all[:, first:last] = jnp.zeros((LINE, count, 256), BF16)
-    relay(2)
+    relay(1, 2)
+    relay(0, 2)
+    w_right[1].wait_recv()
+    swap(1, 1)
+    w_left[0].wait_recv()
+    swap(2, 0)
 
     def normalise(first, last):
         for r in range(first, last, CAP):
@@ -377,17 +390,15 @@
     for copy in tail_copies + w_twin:
         copy.wait_recv()
     forward(*NEAR, 0, LINE - 1)
-    ring[1, -1, 2].wait_recv()
-    pass_on(1, -1, 3)
-    ring[0, 1, 2].wait_recv()
-    pass_on(0, 1, 3)
+    relay_last(1)
+    normed_t[0] = normed[0 : FAR[0]].T
+    cot_t[0] = cot_all[0 : FAR[0]].T
     first_twins = len(w_twin)
     w_far_a.wait_recv()
     swap(3, 0)
     w_far_b.wait_recv()
     swap(3, 1)
-    normed_t[0] = normed[0 : FAR[0]].T
-    cot_t[0] = cot_all[0 : FAR[0]].T
+    relay_last(0)
     for copy in w_twin[first_twins:]:
         copy.wait_recv()
     forward(*NEAR, LINE - 1, LINE)
@@ -398,37 +409,30 @@
         return carry
 
     lax.fori_loop(0, LINE, near_product, 0)
-    backward(*NEAR)
-    for step in (2, -2, 1, -1):
-        y_send(step)
-
-    ring[1, 1, 2].wait_recv()
-    ring[0, -1, 2].wait_recv()
-    ring[1, -1, 3].wait_recv()
-    ring[0, 1, 3].wait_recv()
+
+    for direction in (1, -1):
+        ring[1, direction, 3].wait_recv()
+    cot_t[1] = cot_all[FAR[0] : ROWS].T
+    for direction in (1, -1):
+        ring[0, direction, 3].wait_recv()
     normalise(*FAR)
     forward(*FAR, 0, LINE)
     normed_t[1] = normed[FAR[0] : ROWS].T
-    cot_t[1] = cot_all[FAR[0] : ROWS].T
-
-    def far_product(start, slot):
-        wide = dot(normed_t[1, pl.ds(start, half)], cots_all[slot, FAR[0] : ROWS])
-        narrow = dot(cot_t[1, pl.ds(start, half)], act_all[slot, FAR[0] : ROWS])
-        return (
-            wide + g_acc[slot, pl.ds(start, half), 0:256],
-            narrow + g_acc[slot, pl.ds(start, half), 256:384],
-        )
-
-    their_start = pl.multiple_of((1 - core) * half, half)
-    our_start = pl.multiple_of(core * half, half)
-
-    def theirs(slot, carry):
-        wide, narrow = far_product(their_start, slot)
-        g_out[slot, :, 0:256] = wide.astype(BF16)
-        g_out[slot, :, 256:384] = narrow.astype(BF16)
-        return carry
-
-    lax.fori_loop(0, LINE, theirs, 0)
+
+    def far_product(start, count, slot):
+        some = pl.ds(pl.multiple_of(start, 128), count)
+        wide = dot(normed_t[1, some], cots_all[slot, FAR[0] : ROWS])
+        narrow = dot(cot_t[1, some], act_all[slot, FAR[0] : ROWS])
+        return wide + g_acc[slot, some, 0:256], narrow + g_acc[slot, some, 256:384]
+
+    def theirs(low, high):
+        def block(slot, carry):
+            wide, narrow = far_product((1 - core) * half + low, high - low, slot)
+            g_out[slot, low:high, 0:256] = wide.astype(BF16)
+            g_out[slot, low:high, 256:384] = narrow.astype(BF16)
+            return carry
+
+        lax.fori_loop(0, LINE, block, 0)
 
     def cut(part):
         return slice(PIECES[part], PIECES[part + 1])
@@ -438,17 +442,25 @@
         mid = (first + last) // 2
         return slice(first, mid), slice(mid, last)
 
-    pair_copies = [
-        send(g_out.at[:, cut(part)], g_in.at[:, cut(part)], sibling) for part in range(PARTS)
-    ]
+    def pair(part):
+        return send(g_out.at[:, cut(part)], g_in.at[:, cut(part)], sibling)
+
+    theirs(0, PIECES[1])
+    pair_copies = [pair(0)]
+    theirs(PIECES[1], half)
+    pair_copies += [pair(part) for part in range(1, PARTS)]
 
     def ours(slot, carry):
-        wide, narrow = far_product(our_start, slot)
-        g_acc[slot, pl.ds(our_start, half), 0:256] = wide
-        g_acc[slot, pl.ds(our_start, half), 256:384] = narrow
+        wide, narrow = far_product(core * half, half, slot)
+        some = pl.ds(pl.multiple_of(core * half, half), half)
+        g_acc[slot, some, 0:256] = wide
+        g_acc[slot, some, 256:384] = narrow
         return carry
 
     lax.fori_loop(0, LINE, ours, 0)
+    backward(*NEAR)
+    for step in (2, -2, 1, -1):
+        y_send(step)
 
     x_first, x_second, z_first, z_near, z_far, last_copies = ({} for _ in range(6))
 
@@ -526,7 +538,7 @@
             z_near[part][side].wait_recv()
             theirs = final.at[z_final(part, -2 * step)]
             copies.append(send(theirs, theirs, z_dev(step)))
-            if side == min(part, 1):
+            if side == (0 if part == 1 else 1):
                 copies.append(send(theirs, theirs, z_dev(2 * step)))
         z_far[part] = copies
 

time: 85.4 us -> 86 us (level)
  no operation moved by 1% of the time
where the time goes in v4:
time: 86 us; the launch traced here: 85.8 us
  Pallas kernels  85.1 us (99%)
    pallas_call x1, Pallas kernels, body(): pl.pallas_call(kernel, out_shape=(jax.ShapeDtypeStruct((rows, width), BF1...  82.3 us
    pallas_call x1, Pallas kernels, body(): pl.pallas_call(finish, out_shape=(jax.ShapeDtypeStruct((rows, width), BF1...  2.82 us

profile of v4, /device:TPU:1, one launch (start us, length us, event | category | flops | bytes accessed | tf_op | source)
XLA Modules:
  0.0 85.8 jit_solution(14366135766635549265)
XLA Ops:
  0.6 82.3 %shard_map.129 = (bf16[128,1024]{1,0:T(8,128)(2,1)}, bf16[1024,384]{1,0:T(8,128)(2,1)}, f32[1024,128]{1,0:T(8,128)}, f32[8,256]{1,0:T(8,128)}) custom-call(bf16[128,1024]{1,0:T(8,128)(2,1)} %bitcast.6, s32[1,128]{1,0:T(1,128)} %marks_hbm.1, bf16[8,128]{1,0:T(8,128)(2,1)} %bitcast.9, bf16[4,1024]{1,0:T(4,128)(2,1)} %conv_hbm.1, bf16[8,128]{1,0:T(8,128)(2,1)} %bitcast.10, ...), custom_call_target="tpu_custom_call" | custom-call | tf_op jit(solution)/shard_map/pallas_call | solution.py:750
  83.0 2.8 %shard_map.130 = (bf16[128,1024]{1,0:T(8,128)(2,1)}, f32[2048,128]{1,0:T(8,128)}, f32[2048,128]{1,0:T(8,128)}, f32[128,1024]{1,0:T(8,128)}) custom-call(bf16[128,1024]{1,0:T(8,128)(2,1)} %get-tuple-element.12.bg_hbm, bf16[1024,384]{1,0:T(8,128)(2,1)} %get-tuple-element.13.final_hbm, f32[1024,128]{1,0:T(8,128)} %get-tuple-element.14.tail_hbm, ...), custom_call_target="tpu_custom_call" | custom-call | tf_op jit(solution)/shard_map/pallas_call | solution.py:782

commit v5 on v4

--- a/solution.py
+++ b/solution.py
@@ -13,7 +13,7 @@
 CAP = 48
 EPS = 1e-05
 LINE = 4
-PIECES = (0, 128, 384, 512)
+PIECES = (0, 256, 512)
 PARTS = len(PIECES) - 1
 CHUNK = 32
 
@@ -60,7 +60,6 @@
     bg_ref,
     final,
     tail_b,
-    v_ref,
     x_ref,
     marks_ref,
     enc_gain_ref,
@@ -94,9 +93,8 @@
     y_in,
     v_out,
     v_in,
-    v_pair,
-    v_sib,
-    v_all,
+    v_step,
+    v_other,
     g_acc,
     g_out,
     g_in,
@@ -217,15 +215,17 @@
         copy.wait()
     w_all[0, :, 256:384] = dw_ref[...].astype(F32).T.astype(BF16)
 
-    def w_rows(slot, part):
+    def w_rows(slot):
+        return w_all.at[slot, pl.ds(pl.multiple_of(core * half, half), half)]
+
+    def w_part(slot, part):
         start = pl.multiple_of(core * half + part * (half // 2), half // 2)
         return w_all.at[slot, pl.ds(start, half // 2)]
 
-    w_right = [None, None]
-    w_left = [None, None]
-    for part in (0, 1):
-        w_right[part] = send(w_rows(0, part), w_rows(1, part), x_dev(1))
-        w_left[1 - part] = send(w_rows(0, 1 - part), w_rows(2, 1 - part), x_dev(-1))
+    w_near = [
+        send(w_rows(0), w_rows(1), x_dev(1)),
+        send(w_rows(0), w_rows(2), x_dev(-1)),
+    ]
 
     ring = {}
 
@@ -248,30 +248,36 @@
     load_x.wait()
     enc_gain = as_row(enc_gain_ref[...])
     taps = [conv_ref[tap : tap + 1, :].astype(F32) for tap in range(KW)]
-    for r in range(0, rows, CHUNK):
-        value = x_ref[r : r + CHUNK].astype(F32)
+    def chunk(index):
+        return pl.ds(pl.multiple_of(index * CHUNK, CHUNK), CHUNK)
+
+    def enc_norm(index, carry):
+        value = x_ref[chunk(index)].astype(F32)
         inverse = lax.rsqrt(jnp.mean(value * value, axis=1, keepdims=True) + EPS)
-        inv_x[r : r + CHUNK] = inverse
-        norm_x[16 + r : 16 + r + CHUNK] = value * inverse * enc_gain
+        inv_x[chunk(index)] = inverse
+        norm_x[pl.ds(pl.multiple_of(16 + index * CHUNK, 16), CHUNK)] = value * inverse * enc_gain
+        return carry
+
+    lax.fori_loop(0, rows // CHUNK, enc_norm, 0)
     halo_copy.wait_recv()
     value = halo[...].astype(F32) * (seq > 0).astype(F32)
     inverse = lax.rsqrt(jnp.mean(value * value, axis=1, keepdims=True) + EPS)
     norm_x[0:16] = value * inverse * enc_gain
-    for r in range(0, rows, CHUNK):
-        mixed = taps[0] * norm_x[16 + r : 16 + r + CHUNK]
+
+    def enc_mix(index, carry):
+        block = norm_x[pl.ds(pl.multiple_of(index * CHUNK, CHUNK), CHUNK + 16)]
+        mixed = taps[0] * block[16:]
         for tap in range(1, KW):
-            mixed = mixed + taps[tap] * norm_x[16 + r - tap : 16 + r - tap + CHUNK]
+            mixed = mixed + taps[tap] * block[16 - tap : 16 - tap + CHUNK]
         sigma = jax.nn.sigmoid(mixed)
-        enc_out[r : r + CHUNK] = (x_ref[r : r + CHUNK].astype(F32) + mixed * sigma).astype(BF16)
-        slope[r : r + CHUNK] = sigma * (1.0 + mixed * (1.0 - sigma))
+        enc_out[chunk(index)] = (x_ref[chunk(index)].astype(F32) + mixed * sigma).astype(BF16)
+        slope[chunk(index)] = sigma * (1.0 + mixed * (1.0 - sigma))
+        return carry
+
+    lax.fori_loop(0, rows // CHUNK, enc_mix, 0)
     in_all[0:CAP] = dot(chosen, enc_out[...]).astype(BF16)
     pass_on(0, 1, 0)
     pass_on(0, -1, 0)
-
-    w_twin = []
-
-    def swap(slot, part):
-        w_twin.append(send(w_rows(slot, part), w_rows(slot, part), sibling))
 
     for copy in load_tail:
         copy.wait()
@@ -297,27 +303,21 @@
             ring[which, direction, step - 1].wait_recv()
             pass_on(which, direction, step)
 
-    def relay_last(which):
+    def relay_last(which, direction):
         buffer = (in_all, cot_all)[which]
-        there = Y_ROW[Y_ORDER.index(4)]
-        for direction in (1, -1):
-            ring[which, direction, 2].wait_recv()
-            here = Y_ROW[Y_ORDER.index(-3 * direction)]
-            lanes = slice(0, half) if direction == 1 else slice(half, width)
-            ring[which, direction, 3] = send(
-                buffer.at[here : here + CAP, lanes],
-                buffer.at[there : there + CAP, lanes],
-                y_dev(direction),
-            )
+        here, there = (Y_ROW[Y_ORDER.index(rel)] for rel in (-3 * direction, 4))
+        ring[which, direction, 2].wait_recv()
+        ring[which, direction, 3] = send(
+            buffer.at[here : here + CAP], buffer.at[there : there + CAP], y_dev(direction)
+        )
 
     relay(1, 1)
     relay(0, 1)
-    w_right[0].wait_recv()
-    w_far_a = send(w_rows(1, 0), w_rows(3, 0), x_dev(1))
-    w_left[1].wait_recv()
-    w_far_b = send(w_rows(2, 1), w_rows(3, 1), x_dev(-1))
-    swap(1, 0)
-    swap(2, 1)
+    w_near[0].wait_recv()
+    w_far = [send(w_part(1, 0), w_part(3, 0), x_dev(1))]
+    w_near[1].wait_recv()
+    w_far.append(send(w_part(2, 1), w_part(3, 1), x_dev(-1)))
+    w_twin = [send(w_rows(slot), w_rows(slot), sibling) for slot in (1, 2)]
     for first, last in ((NEAR[1], FAR[0]), (FAR[1], ROWS)):
         count = last - first
         normed[first:last] = jnp.zeros((count, width), BF16)
@@ -327,21 +327,21 @@
         cots_all[:, first:last] = jnp.zeros((LINE, count, 256), BF16)
     relay(1, 2)
     relay(0, 2)
-    w_right[1].wait_recv()
-    swap(1, 1)
-    w_left[0].wait_recv()
-    swap(2, 0)
 
     def normalise(first, last):
-        for r in range(first, last, CAP):
-            head = in_all[r : r + CAP].astype(F32)
+        def block(index, carry):
+            some = pl.ds(pl.multiple_of(first + index * CAP, 16), CAP)
+            head = in_all[some].astype(F32)
             square = jnp.sum(head * head, axis=1, keepdims=True) + tail_square
             inverse = lax.rsqrt(square / (2 * width) + EPS)
-            inv_all[r : r + CAP] = inverse
-            normed[r : r + CAP] = (head * inverse * gain_head).astype(BF16)
+            inv_all[some] = inverse
+            normed[some] = (head * inverse * gain_head).astype(BF16)
+            return carry
+
+        lax.fori_loop(0, (last - first) // CAP, block, 0)
         tin_all[first:last] = jnp.zeros((last - first, 1), F32)
 
-    def forward(first, last, low, high):
+    def forward(first, last):
         def block(slot, carry):
             tail = tails[slot, 0:1, :]
             both = dot(normed[first:last], w_all[slot, :, 0:256]) + inv_all[first:last] * tail
@@ -361,23 +361,29 @@
             )
             return carry
 
-        lax.fori_loop(low, high, block, 0)
-
-    def backward(first, last):
-        def block(slot, carry):
-            back[first:last] += dot_lanes(cots_all[slot, first:last], w_all[slot, :, 0:256])
+        lax.fori_loop(0, LINE, block, 0)
+
+    def backward():
+        def features(index, carry):
+            some = pl.ds(pl.multiple_of(index * 256, 256), 256)
+            total = dot_lanes(cots_all[0, 0 : FAR[1]], w_all[0, some, 0:256])
+            for slot in range(1, LINE):
+                total = total + dot_lanes(cots_all[slot, 0 : FAR[1]], w_all[slot, some, 0:256])
+            back[0 : FAR[1], some] = total
             return carry
 
-        back[first:last] = dot_lanes(cots_all[0, first:last], w_all[0, :, 0:256])
-        lax.fori_loop(1, LINE, block, 0)
-        for r in range(first, last, CAP):
-            inverse = inv_all[r : r + CAP]
-            unit = in_all[r : r + CAP].astype(F32) * inverse
-            scaled = back[r : r + CAP] * gain_head
-            inner = jnp.sum(scaled * unit, axis=1, keepdims=True) + tin_all[r : r + CAP] * inverse
-            part_all[r : r + CAP] = (
-                (scaled - unit * (inner / (2 * width))) * inverse
-            ).astype(BF16)
+        lax.fori_loop(0, width // 256, features, 0)
+
+        def block(index, carry):
+            some = pl.ds(pl.multiple_of(index * 16, 16), 16)
+            inverse = inv_all[some]
+            unit = in_all[some].astype(F32) * inverse
+            scaled = back[some] * gain_head
+            inner = jnp.sum(scaled * unit, axis=1, keepdims=True) + tin_all[some] * inverse
+            part_all[some] = ((scaled - unit * (inner / (2 * width))) * inverse).astype(BF16)
+            return carry
+
+        lax.fori_loop(0, FAR[1] // 16, block, 0)
 
     y_copies = []
 
@@ -387,21 +393,16 @@
         y_copies.append(send(part_all.at[row : row + CAP], y_in.at[there], y_dev(step)))
 
     normalise(*NEAR)
+    normed_t[0] = normed[0 : FAR[0]].T
+    cot_t[0] = cot_all[0 : FAR[0]].T
+    relay_last(1, -1)
+    for copy in w_far:
+        copy.wait_recv()
+    w_twin.append(send(w_rows(3), w_rows(3), sibling))
+    relay_last(0, 1)
     for copy in tail_copies + w_twin:
         copy.wait_recv()
-    forward(*NEAR, 0, LINE - 1)
-    relay_last(1)
-    normed_t[0] = normed[0 : FAR[0]].T
-    cot_t[0] = cot_all[0 : FAR[0]].T
-    first_twins = len(w_twin)
-    w_far_a.wait_recv()
-    swap(3, 0)
-    w_far_b.wait_recv()
-    swap(3, 1)
-    relay_last(0)
-    for copy in w_twin[first_twins:]:
-        copy.wait_recv()
-    forward(*NEAR, LINE - 1, LINE)
+    forward(*NEAR)
 
     def near_product(slot, carry):
         g_acc[slot, :, 0:256] = dot(normed_t[0], cots_all[slot, 0 : FAR[0]])
@@ -410,13 +411,13 @@
 
     lax.fori_loop(0, LINE, near_product, 0)
 
-    for direction in (1, -1):
-        ring[1, direction, 3].wait_recv()
+    ring[1, 1, 2].wait_recv()
+    ring[1, -1, 3].wait_recv()
     cot_t[1] = cot_all[FAR[0] : ROWS].T
-    for direction in (1, -1):
-        ring[0, direction, 3].wait_recv()
+    ring[0, -1, 2].wait_recv()
+    ring[0, 1, 3].wait_recv()
     normalise(*FAR)
-    forward(*FAR, 0, LINE)
+    forward(*FAR)
     normed_t[1] = normed[FAR[0] : ROWS].T
 
     def far_product(start, count, slot):
@@ -425,14 +426,13 @@
         narrow = dot(cot_t[1, some], act_all[slot, FAR[0] : ROWS])
         return wide + g_acc[slot, some, 0:256], narrow + g_acc[slot, some, 256:384]
 
-    def theirs(low, high):
-        def block(slot, carry):
-            wide, narrow = far_product((1 - core) * half + low, high - low, slot)
-            g_out[slot, low:high, 0:256] = wide.astype(BF16)
-            g_out[slot, low:high, 256:384] = narrow.astype(BF16)
-            return carry
-
-        lax.fori_loop(0, LINE, block, 0)
+    def theirs(slot, carry):
+        wide, narrow = far_product((1 - core) * half, half, slot)
+        g_out[slot, :, 0:256] = wide.astype(BF16)
+        g_out[slot, :, 256:384] = narrow.astype(BF16)
+        return carry
+
+    lax.fori_loop(0, LINE, theirs, 0)
 
     def cut(part):
         return slice(PIECES[part], PIECES[part + 1])
@@ -442,13 +442,9 @@
         mid = (first + last) // 2
         return slice(first, mid), slice(mid, last)
 
-    def pair(part):
-        return send(g_out.at[:, cut(part)], g_in.at[:, cut(part)], sibling)
-
-    theirs(0, PIECES[1])
-    pair_copies = [pair(0)]
-    theirs(PIECES[1], half)
-    pair_copies += [pair(part) for part in range(1, PARTS)]
+    pair_copies = [
+        send(g_out.at[:, cut(part)], g_in.at[:, cut(part)], sibling) for part in range(PARTS)
+    ]
 
     def ours(slot, carry):
         wide, narrow = far_product(core * half, half, slot)
@@ -458,9 +454,6 @@
         return carry
 
     lax.fori_loop(0, LINE, ours, 0)
-    backward(*NEAR)
-    for step in (2, -2, 1, -1):
-        y_send(step)
 
     x_first, x_second, z_first, z_near, z_far, last_copies = ({} for _ in range(6))
 
@@ -538,7 +531,7 @@
             z_near[part][side].wait_recv()
             theirs = final.at[z_final(part, -2 * step)]
             copies.append(send(theirs, theirs, z_dev(step)))
-            if side == (0 if part == 1 else 1):
+            if side == part:
                 copies.append(send(theirs, theirs, z_dev(2 * step)))
         z_far[part] = copies
 
@@ -550,11 +543,10 @@
 
     x_start(0)
     x_start(1)
-    backward(*FAR)
-    for step in (4, 3, -3):
+    backward()
+    for step in (4, 3, -3, 2, -2, 1, -1):
         y_send(step)
     x_relay(0)
-    x_start(2)
     x_relay(1)
 
     def tail_rows(slot, carry):
@@ -568,23 +560,34 @@
         send(v_out.at[2], v_in.at[1], x_dev(1)),
         send(v_out.at[3], v_in.at[2], x_dev(2)),
     ]
-    x_relay(2)
     z_start(0)
 
     for copy in v_copies:
         copy.wait_recv()
-    v_pair[...] = v_out[0] + v_in[0] + v_in[1] + v_in[2]
-    v_swap = send(v_pair, v_sib, sibling)
-
+    v_step[0] = v_out[0] + v_in[0] + v_in[1] + v_in[2]
+    v_peers = [sibling] + [
+        {"dp": (z + size - 2 * size * ((z // size) % 2)) * 2 + core} for size in (1, 2, 4)
+    ]
+
+    def v_send(index):
+        return send(v_step.at[index], v_other.at[index], v_peers[index])
+
+    def v_join(index, copy):
+        copy.wait_recv()
+        v_step[index + 1] = v_step[index] + v_other[index]
+
+    v_copy = v_send(0)
     z_start(1)
-    v_swap.wait_recv()
-    v_all[z] = v_pair[...] + v_sib[...]
-    v_spread = [send(v_all.at[z], v_all.at[z], z_dev(step)) for step in range(1, n_z)]
+    v_join(0, v_copy)
+    v_copy = v_send(1)
     z_sum(0)
-    z_start(2)
+    v_join(1, v_copy)
+    v_copy = v_send(2)
+    z_spread(0)
+    v_join(2, v_copy)
+    v_copy = v_send(3)
     z_sum(1)
-    z_spread(0)
-    z_sum(2)
+    z_end(0)
     z_spread(1)
     early = len(started)
 
@@ -595,40 +598,33 @@
         widen_cot = widen_cot + y_in[index].astype(F32)
     spread = dot_rows(chosen, cot_all[0:CAP]) + dot_rows(chosen, widen_cot.astype(BF16))
     ecot[...] = oc_ref[...].astype(F32) + spread
-    for r in range(0, rows, CHUNK):
-        g_mix[r : r + CHUNK] = ecot[r : r + CHUNK] * slope[r : r + CHUNK]
+    g_mix[0:rows] = ecot[...] * slope[...]
     edge_copy = send(g_mix.at[0:8], edge, before)
-
-    z_spread(2)
-    z_end(0)
 
     edge_copy.wait_recv()
     g_mix[rows : rows + 8] = edge[...] * (seq < n_seq - 1).astype(F32)
-    for r in range(0, rows, CHUNK):
-        grad = taps[0] * g_mix[r : r + CHUNK]
+
+    def enc_back(index, carry):
+        block = g_mix[pl.ds(pl.multiple_of(index * CHUNK, CHUNK), CHUNK + 8)]
+        grad = taps[0] * block[0:CHUNK]
         for tap in range(1, KW):
-            grad = grad + taps[tap] * g_mix[r + tap : r + tap + CHUNK]
+            grad = grad + taps[tap] * block[tap : tap + CHUNK]
         grad = grad * enc_gain
-        value = x_ref[r : r + CHUNK].astype(F32)
-        inverse = inv_x[r : r + CHUNK]
+        value = x_ref[chunk(index)].astype(F32)
+        inverse = inv_x[chunk(index)]
         inner = jnp.mean(grad * value, axis=1, keepdims=True) * (inverse * inverse)
-        bg_ref[r : r + CHUNK] = (
-            ecot[r : r + CHUNK] + (grad - value * inner) * inverse
-        ).astype(BF16)
+        bg_ref[chunk(index)] = (ecot[chunk(index)] + (grad - value * inner) * inverse).astype(BF16)
+        return carry
+
+    lax.fori_loop(0, rows // CHUNK, enc_back, 0)
     store(bg_ref, bg_hbm)
 
-    for copy in v_spread:
-        copy.wait_recv()
-    v_total = v_all[0]
-    for chip in range(1, n_z):
-        v_total = v_total + v_all[chip]
-    v_ref[...] = v_total
-    store(v_ref, v_hbm)
-
-    z_end(1)
+    v_join(3, v_copy)
+    store(v_step.at[4], v_hbm)
+
     for copy in started[:early]:
         copy.wait_send()
-    z_end(2)
+    z_end(1)
     for part in range(PARTS):
         store(final.at[own_rows(part)], final_hbm.at[own_rows(part)])
     for part in range(PARTS):
@@ -698,7 +694,6 @@
         ((rows, width), BF16),
         ((width, 384), BF16),
         ((width, 128), F32),
-        ((8, 256), F32),
         ((rows, width), BF16),
         ((1, rows), jnp.int32),
         ((8, width // 8), BF16),
@@ -732,9 +727,8 @@
         ((n_y, CAP, width), BF16),
         ((LINE, 8, 256), F32),
         ((LINE - 1, 8, 256), F32),
-        ((8, 256), F32),
-        ((8, 256), F32),
-        ((n_z, 8, 256), F32),
+        ((5, 8, 256), F32),
+        ((4, 8, 256), F32),
         ((LINE, width, 384), F32),
         ((LINE, half, 384), BF16),
         ((LINE, half, 384), BF16),
@@ -761,8 +755,8 @@
         + [
             pltpu.SemaphoreType.DMA((12,)),
             pltpu.SemaphoreType.DMA((9,)),
-            pltpu.SemaphoreType.DMA((120,)),
-            pltpu.SemaphoreType.DMA((120,)),
+            pltpu.SemaphoreType.DMA((96,)),
+            pltpu.SemaphoreType.DMA((96,)),
         ],
         compiler_params=pltpu.CompilerParams(
             collective_id=0, has_side_effects=True, vmem_limit_bytes=60 * 1024 * 1024

time: 86 us -> 87.7 us (1.020)
  Pallas kernels: 85.1 us -> 86.9 us
    pallas_call x1, Pallas kernels: 82.3 us -> 84.1 us  [body(): pl.pallas_call(kernel, out_shape=(jax.ShapeDtypeStruct((rows, width), BF1...]
where the time goes in v5:
time: 87.7 us; the launch traced here: 87.6 us
  Pallas kernels  86.9 us (99%)
    pallas_call x1, Pallas kernels, body(): pl.pallas_call(kernel, out_shape=(jax.ShapeDtypeStruct((rows, width), BF1...  84.1 us
    pallas_call x1, Pallas kernels, body(): pl.pallas_call(finish, out_shape=(jax.ShapeDtypeStruct((rows, width), BF1...  2.82 us

profile of v5, /device:TPU:1, one launch (start us, length us, event | category | flops | bytes accessed | tf_op | source)
XLA Modules:
  0.0 87.6 jit_solution(5246980066095402701)
XLA Ops:
  0.6 84.1 %shard_map.129 = (bf16[128,1024]{1,0:T(8,128)(2,1)}, bf16[1024,384]{1,0:T(8,128)(2,1)}, f32[1024,128]{1,0:T(8,128)}, f32[8,256]{1,0:T(8,128)}) custom-call(bf16[128,1024]{1,0:T(8,128)(2,1)} %bitcast.6, s32[1,128]{1,0:T(1,128)} %marks_hbm.1, bf16[8,128]{1,0:T(8,128)(2,1)} %bitcast.9, bf16[4,1024]{1,0:T(4,128)(2,1)} %conv_hbm.1, bf16[8,128]{1,0:T(8,128)(2,1)} %bitcast.10, ...), custom_call_target="tpu_custom_call" | custom-call | tf_op jit(solution)/shard_map/pallas_call | solution.py:744
  84.7 2.8 %shard_map.130 = (bf16[128,1024]{1,0:T(8,128)(2,1)}, f32[2048,128]{1,0:T(8,128)}, f32[2048,128]{1,0:T(8,128)}, f32[128,1024]{1,0:T(8,128)}) custom-call(bf16[128,1024]{1,0:T(8,128)(2,1)} %get-tuple-element.12.bg_hbm, bf16[1024,384]{1,0:T(8,128)(2,1)} %get-tuple-element.13.final_hbm, f32[1024,128]{1,0:T(8,128)} %get-tuple-element.14.tail_hbm, ...), custom_call_target="tpu_custom_call" | custom-call | tf_op jit(solution)/shard_map/pallas_call | solution.py:776

commit v6 on v4

--- a/solution.py
+++ b/solution.py
@@ -13,7 +13,7 @@
 CAP = 48
 EPS = 1e-05
 LINE = 4
-PIECES = (0, 128, 384, 512)
+PIECES = (0, 256, 384, 512)
 PARTS = len(PIECES) - 1
 CHUNK = 32
 
@@ -223,9 +223,12 @@
 
     w_right = [None, None]
     w_left = [None, None]
-    for part in (0, 1):
+
+    def w_send(part):
         w_right[part] = send(w_rows(0, part), w_rows(1, part), x_dev(1))
         w_left[1 - part] = send(w_rows(0, 1 - part), w_rows(2, 1 - part), x_dev(-1))
+
+    w_send(0)
 
     ring = {}
 
@@ -236,12 +239,6 @@
         ring[which, direction, step] = send(
             buffer.at[here : here + CAP], buffer.at[there : there + CAP], y_dev(direction)
         )
-
-    lead_copy.wait_recv()
-    carried = lead_in[0:1] * (seq < n_seq - 1).astype(F32)
-    cot_all[0:CAP] = (own_sums + last_slot * carried).astype(BF16)
-    pass_on(1, 1, 0)
-    pass_on(1, -1, 0)
 
     load_gain.wait()
     load_conv.wait()
@@ -253,6 +250,12 @@
         inverse = lax.rsqrt(jnp.mean(value * value, axis=1, keepdims=True) + EPS)
         inv_x[r : r + CHUNK] = inverse
         norm_x[16 + r : 16 + r + CHUNK] = value * inverse * enc_gain
+    lead_copy.wait_recv()
+    carried = lead_in[0:1] * (seq < n_seq - 1).astype(F32)
+    cot_all[0:CAP] = (own_sums + last_slot * carried).astype(BF16)
+    pass_on(1, 1, 0)
+    pass_on(1, -1, 0)
+
     halo_copy.wait_recv()
     value = halo[...].astype(F32) * (seq > 0).astype(F32)
     inverse = lax.rsqrt(jnp.mean(value * value, axis=1, keepdims=True) + EPS)
@@ -267,6 +270,7 @@
     in_all[0:CAP] = dot(chosen, enc_out[...]).astype(BF16)
     pass_on(0, 1, 0)
     pass_on(0, -1, 0)
+    w_send(1)
 
     w_twin = []
 
@@ -459,8 +463,6 @@
 
     lax.fori_loop(0, LINE, ours, 0)
     backward(*NEAR)
-    for step in (2, -2, 1, -1):
-        y_send(step)
 
     x_first, x_second, z_first, z_near, z_far, last_copies = ({} for _ in range(6))
 
@@ -530,7 +532,8 @@
             total = total + z_in[index, z_slot(part)].astype(F32)
         final[z_final(part, 0)] = total.astype(BF16)
         mine = final.at[z_final(part, 0)]
-        z_near[part] = [send(mine, mine, z_dev(step)) for step in (2, -2, 1, -1)]
+        steps = (2, -2, 1, -1) if part < PARTS - 1 else (4, 3, -3, 2, -2, 1, -1)
+        z_near[part] = [send(mine, mine, z_dev(step)) for step in steps]
 
     def z_spread(part):
         copies = []
@@ -538,23 +541,26 @@
             z_near[part][side].wait_recv()
             theirs = final.at[z_final(part, -2 * step)]
             copies.append(send(theirs, theirs, z_dev(step)))
-            if side == (0 if part == 1 else 1):
+            if side == min(part, 1):
                 copies.append(send(theirs, theirs, z_dev(2 * step)))
         z_far[part] = copies
 
     def z_end(part):
-        for copy in z_near[part][2:] + z_far[part]:
+        waits = z_near[part][2:] + z_far[part] if part < PARTS - 1 else z_near[part]
+        for copy in waits:
             copy.wait_recv()
         mine = final.at[own_rows(part)]
         last_copies[part] = send(mine, mine, sibling)
 
     x_start(0)
     x_start(1)
+    for step in (2, -2):
+        y_send(step)
     backward(*FAR)
-    for step in (4, 3, -3):
-        y_send(step)
     x_relay(0)
     x_start(2)
+    for step in (4, 3, -3, 1, -1):
+        y_send(step)
     x_relay(1)
 
     def tail_rows(slot, carry):
@@ -599,7 +605,6 @@
         g_mix[r : r + CHUNK] = ecot[r : r + CHUNK] * slope[r : r + CHUNK]
     edge_copy = send(g_mix.at[0:8], edge, before)
 
-    z_spread(2)
     z_end(0)
 
     edge_copy.wait_recv()

time: 86 us -> 84.5 us (0.983)
  Pallas kernels: 85.1 us -> 83.7 us
    pallas_call x1, Pallas kernels: 82.3 us -> 80.9 us  [body(): pl.pallas_call(kernel, out_shape=(jax.ShapeDtypeStruct((rows, width), BF1...]
where the time goes in v6:
time: 84.5 us; the launch traced here: 84.3 us
  Pallas kernels  83.7 us (99%)
    pallas_call x1, Pallas kernels, body(): pl.pallas_call(kernel, out_shape=(jax.ShapeDtypeStruct((rows, width), BF1...  80.9 us
    pallas_call x1, Pallas kernels, body(): pl.pallas_call(finish, out_shape=(jax.ShapeDtypeStruct((rows, width), BF1...  2.82 us

profile of v6, /device:TPU:1, one launch (start us, length us, event | category | flops | bytes accessed | tf_op | source)
XLA Modules:
  0.0 84.3 jit_solution(3075158796997271250)
XLA Ops:
  0.6 80.9 %shard_map.129 = (bf16[128,1024]{1,0:T(8,128)(2,1)}, bf16[1024,384]{1,0:T(8,128)(2,1)}, f32[1024,128]{1,0:T(8,128)}, f32[8,256]{1,0:T(8,128)}) custom-call(bf16[128,1024]{1,0:T(8,128)(2,1)} %bitcast.6, s32[1,128]{1,0:T(1,128)} %marks_hbm.1, bf16[8,128]{1,0:T(8,128)(2,1)} %bitcast.9, bf16[4,1024]{1,0:T(4,128)(2,1)} %conv_hbm.1, bf16[8,128]{1,0:T(8,128)(2,1)} %bitcast.10, ...), custom_call_target="tpu_custom_call" | custom-call | tf_op jit(solution)/shard_map/pallas_call | solution.py:755
  81.5 2.8 %shard_map.130 = (bf16[128,1024]{1,0:T(8,128)(2,1)}, f32[2048,128]{1,0:T(8,128)}, f32[2048,128]{1,0:T(8,128)}, f32[128,1024]{1,0:T(8,128)}) custom-call(bf16[128,1024]{1,0:T(8,128)(2,1)} %get-tuple-element.12.bg_hbm, bf16[1024,384]{1,0:T(8,128)(2,1)} %get-tuple-element.13.final_hbm, f32[1024,128]{1,0:T(8,128)} %get-tuple-element.14.tail_hbm, ...), custom_call_target="tpu_custom_call" | custom-call | tf_op jit(solution)/shard_map/pallas_call | solution.py:787

commit v7 on v6

--- a/solution.py
+++ b/solution.py
@@ -92,6 +92,9 @@
     back,
     part_all,
     y_in,
+    y_relay,
+    y_cross,
+    y_mid,
     v_out,
     v_in,
     v_pair,
@@ -170,7 +173,7 @@
         return copy
 
     barrier = pltpu.get_barrier_semaphore()
-    peers = [y_dev(step) for step in range(1, n_y)]
+    peers = [y_dev(step) for step in (1, -1, 2, -2)]
     peers += [x_dev(step) for step in (1, -1, 2)]
     peers += [z_dev(step) for step in range(1, n_z)]
     peers += [sibling, after, before]
@@ -232,13 +235,21 @@
 
     ring = {}
 
-    def pass_on(which, direction, step):
+    def pass_on(which, side, direction, step):
         buffer = (in_all, cot_all)[which]
+        lanes = slice(side * half, (side + 1) * half)
         here = Y_ROW[Y_ORDER.index(-direction * step)]
-        there = Y_ROW[Y_ORDER.index(-direction * (step + 1))]
-        ring[which, direction, step] = send(
-            buffer.at[here : here + CAP], buffer.at[there : there + CAP], y_dev(direction)
+        there = Y_ROW[Y_ORDER.index(4 if step == 3 else -direction * (step + 1))]
+        ring[which, side, direction, step] = send(
+            buffer.at[here : here + CAP, lanes],
+            buffer.at[there : there + CAP, lanes],
+            y_dev(direction),
         )
+
+    def first_hop(which):
+        for side in (0, 1):
+            for direction in (1, -1):
+                pass_on(which, side, direction, 0)
 
     load_gain.wait()
     load_conv.wait()
@@ -253,8 +264,7 @@
     lead_copy.wait_recv()
     carried = lead_in[0:1] * (seq < n_seq - 1).astype(F32)
     cot_all[0:CAP] = (own_sums + last_slot * carried).astype(BF16)
-    pass_on(1, 1, 0)
-    pass_on(1, -1, 0)
+    first_hop(1)
 
     halo_copy.wait_recv()
     value = halo[...].astype(F32) * (seq > 0).astype(F32)
@@ -268,8 +278,7 @@
         enc_out[r : r + CHUNK] = (x_ref[r : r + CHUNK].astype(F32) + mixed * sigma).astype(BF16)
         slope[r : r + CHUNK] = sigma * (1.0 + mixed * (1.0 - sigma))
     in_all[0:CAP] = dot(chosen, enc_out[...]).astype(BF16)
-    pass_on(0, 1, 0)
-    pass_on(0, -1, 0)
+    first_hop(0)
     w_send(1)
 
     w_twin = []
@@ -297,22 +306,20 @@
     ]
 
     def relay(which, step):
-        for direction in (1, -1):
-            ring[which, direction, step - 1].wait_recv()
-            pass_on(which, direction, step)
+        for side in (0, 1):
+            for direction in (1, -1):
+                ring[which, side, direction, step - 1].wait_recv()
+                pass_on(which, side, direction, step)
 
     def relay_last(which):
-        buffer = (in_all, cot_all)[which]
-        there = Y_ROW[Y_ORDER.index(4)]
-        for direction in (1, -1):
-            ring[which, direction, 2].wait_recv()
-            here = Y_ROW[Y_ORDER.index(-3 * direction)]
-            lanes = slice(0, half) if direction == 1 else slice(half, width)
-            ring[which, direction, 3] = send(
-                buffer.at[here : here + CAP, lanes],
-                buffer.at[there : there + CAP, lanes],
-                y_dev(direction),
-            )
+        for side, direction in ((0, 1), (1, -1)):
+            ring[which, side, direction, 2].wait_recv()
+            pass_on(which, side, direction, 3)
+
+    def wait_last(which):
+        for side, direction in ((0, 1), (1, -1)):
+            ring[which, 1 - side, direction, 2].wait_recv()
+            ring[which, side, direction, 3].wait_recv()
 
     relay(1, 1)
     relay(0, 1)
@@ -383,12 +390,9 @@
                 (scaled - unit * (inner / (2 * width))) * inverse
             ).astype(BF16)
 
-    y_copies = []
-
-    def y_send(step):
+    def part_of(step, lanes=slice(None)):
         row = Y_ROW[Y_ORDER.index(step)]
-        there = Y_ORDER.index(4 if step == 4 else -step)
-        y_copies.append(send(part_all.at[row : row + CAP], y_in.at[there], y_dev(step)))
+        return part_all.at[row : row + CAP, lanes]
 
     normalise(*NEAR)
     for copy in tail_copies + w_twin:
@@ -414,11 +418,9 @@
 
     lax.fori_loop(0, LINE, near_product, 0)
 
-    for direction in (1, -1):
-        ring[1, direction, 3].wait_recv()
+    wait_last(1)
     cot_t[1] = cot_all[FAR[0] : ROWS].T
-    for direction in (1, -1):
-        ring[0, direction, 3].wait_recv()
+    wait_last(0)
     normalise(*FAR)
     forward(*FAR, 0, LINE)
     normed_t[1] = normed[FAR[0] : ROWS].T
@@ -554,13 +556,19 @@
 
     x_start(0)
     x_start(1)
-    for step in (2, -2):
-        y_send(step)
+    y_copies = [
+        send(part_of(1), y_in.at[0], y_dev(1)),
+        send(part_of(-1), y_in.at[1], y_dev(-1)),
+    ]
     backward(*FAR)
     x_relay(0)
     x_start(2)
-    for step in (4, 3, -3, 1, -1):
-        y_send(step)
+    y_relays = [
+        send(part_of(3), y_relay.at[0], y_dev(1)),
+        send(part_of(-3), y_relay.at[1], y_dev(-1)),
+        send(part_of(4, slice(0, half)), y_cross.at[0], y_dev(2)),
+        send(part_of(4, slice(half, width)), y_cross.at[1], y_dev(-2)),
+    ]
     x_relay(1)
 
     def tail_rows(slot, carry):
@@ -586,6 +594,18 @@
     v_swap.wait_recv()
     v_all[z] = v_pair[...] + v_sib[...]
     v_spread = [send(v_all.at[z], v_all.at[z], z_dev(step)) for step in range(1, n_z)]
+
+    for copy in y_relays:
+        copy.wait_recv()
+    for side, step in ((0, 2), (1, -2)):
+        row = Y_ROW[Y_ORDER.index(step)]
+        total = part_all[row : row + CAP].astype(F32) + y_relay[side].astype(F32)
+        lanes = slice(side * half, (side + 1) * half)
+        other = slice((1 - side) * half, (2 - side) * half)
+        y_mid[side, :, lanes] = (total[:, lanes] + y_cross[side].astype(F32)).astype(BF16)
+        y_mid[side, :, other] = total[:, other].astype(BF16)
+        y_copies.append(send(y_mid.at[side], y_in.at[2 + side], y_dev(step)))
+
     z_sum(0)
     z_start(2)
     z_sum(1)
@@ -597,7 +617,7 @@
     for copy in y_copies:
         copy.wait_recv()
     widen_cot = part_all[0:CAP].astype(F32)
-    for index in range(1, n_y):
+    for index in range(4):
         widen_cot = widen_cot + y_in[index].astype(F32)
     spread = dot_rows(chosen, cot_all[0:CAP]) + dot_rows(chosen, widen_cot.astype(BF16))
     ecot[...] = oc_ref[...].astype(F32) + spread
@@ -657,11 +677,17 @@
         copies.append(step)
         return step
 
-    load_final = copy(final_hbm, final)
     load_tail = copy(tail_hbm, tail_b)
     load_v = copy(v_hbm, v_ref)
+    load_final = copy(final_hbm, final)
     load_bg = copy(bg_hbm, bg)
     head, tail = slice(0, width), slice(width, 2 * width)
+    load_tail.wait()
+    load_v.wait()
+    gg[tail] = tail_b[...] * v_ref[0:1, 0:128]
+    copy(gg.at[tail], gg_out.at[tail])
+    ug[tail] = tail_b[...] * v_ref[0:1, 128:256]
+    copy(ug.at[tail], ug_out.at[tail])
     load_final.wait()
     gg[head] = final[:, 0:128].astype(F32)
     copy(gg.at[head], gg_out.at[head])
@@ -669,12 +695,6 @@
     copy(ug.at[head], ug_out.at[head])
     load_bg.wait()
     copy(bg, bg_out)
-    load_tail.wait()
-    load_v.wait()
-    gg[tail] = tail_b[...] * v_ref[0:1, 0:128]
-    copy(gg.at[tail], gg_out.at[tail])
-    ug[tail] = tail_b[...] * v_ref[0:1, 128:256]
-    copy(ug.at[tail], ug_out.at[tail])
     dg[...] = final[:, 256:384].astype(F32).T
     copy(dg, dg_out)
     for step in copies[4:]:
@@ -734,7 +754,10 @@
         ((LINE, ROWS, 256), BF16),
         ((ROWS, width), F32),
         ((ROWS, width), BF16),
-        ((n_y, CAP, width), BF16),
+        ((4, CAP, width), BF16),
+        ((2, CAP, width), BF16),
+        ((2, CAP, half), BF16),
+        ((2, CAP, width), BF16),
         ((LINE, 8, 256), F32),
         ((LINE - 1, 8, 256), F32),
         ((8, 256), F32),
@@ -766,8 +789,8 @@
         + [
             pltpu.SemaphoreType.DMA((12,)),
             pltpu.SemaphoreType.DMA((9,)),
-            pltpu.SemaphoreType.DMA((120,)),
-            pltpu.SemaphoreType.DMA((120,)),
+            pltpu.SemaphoreType.DMA((144,)),
+            pltpu.SemaphoreType.DMA((144,)),
         ],
         compiler_params=pltpu.CompilerParams(
             collective_id=0, has_side_effects=True, vmem_limit_bytes=60 * 1024 * 1024

time: 84.5 us -> 83.5 us (0.988)
  Pallas kernels: 83.7 us -> 82.7 us
    pallas_call x1, Pallas kernels: 80.9 us -> 79.9 us  [body(): pl.pallas_call(kernel, out_shape=(jax.ShapeDtypeStruct((rows, width), BF1...]
where the time goes in v7:
time: 83.5 us; the launch traced here: 83.3 us
  Pallas kernels  82.7 us (99%)
    pallas_call x1, Pallas kernels, body(): pl.pallas_call(kernel, out_shape=(jax.ShapeDtypeStruct((rows, width), BF1...  79.9 us
    pallas_call x1, Pallas kernels, body(): pl.pallas_call(finish, out_shape=(jax.ShapeDtypeStruct((rows, width), BF1...  2.75 us

profile of v7, /device:TPU:1, one launch (start us, length us, event | category | flops | bytes accessed | tf_op | source)
XLA Modules:
  0.0 83.3 jit_solution(4943935369113016815)
XLA Ops:
  0.6 79.9 %shard_map.129 = (bf16[128,1024]{1,0:T(8,128)(2,1)}, bf16[1024,384]{1,0:T(8,128)(2,1)}, f32[1024,128]{1,0:T(8,128)}, f32[8,256]{1,0:T(8,128)}) custom-call(bf16[128,1024]{1,0:T(8,128)(2,1)} %bitcast.6, s32[1,128]{1,0:T(1,128)} %marks_hbm.1, bf16[8,128]{1,0:T(8,128)(2,1)} %bitcast.9, bf16[4,1024]{1,0:T(4,128)(2,1)} %conv_hbm.1, bf16[8,128]{1,0:T(8,128)(2,1)} %bitcast.10, ...), custom_call_target="tpu_custom_call" | custom-call | tf_op jit(solution)/shard_map/pallas_call | solution.py:778
  80.6 2.8 %shard_map.130 = (bf16[128,1024]{1,0:T(8,128)(2,1)}, f32[2048,128]{1,0:T(8,128)}, f32[2048,128]{1,0:T(8,128)}, f32[128,1024]{1,0:T(8,128)}) custom-call(bf16[128,1024]{1,0:T(8,128)(2,1)} %get-tuple-element.12.bg_hbm, bf16[1024,384]{1,0:T(8,128)(2,1)} %get-tuple-element.13.final_hbm, f32[1024,128]{1,0:T(8,128)} %get-tuple-element.14.tail_hbm, ...), custom_call_target="tpu_custom_call" | custom-call | tf_op jit(solution)/shard_map/pallas_call | solution.py:810

commit v8 on v7

--- a/solution.py
+++ b/solution.py
@@ -13,7 +13,7 @@
 CAP = 48
 EPS = 1e-05
 LINE = 4
-PIECES = (0, 256, 384, 512)
+PIECES = (0, 128, 384, 512)
 PARTS = len(PIECES) - 1
 CHUNK = 32
 
@@ -464,7 +464,6 @@
         return carry
 
     lax.fori_loop(0, LINE, ours, 0)
-    backward(*NEAR)
 
     x_first, x_second, z_first, z_near, z_far, last_copies = ({} for _ in range(6))
 
@@ -543,7 +542,7 @@
             z_near[part][side].wait_recv()
             theirs = final.at[z_final(part, -2 * step)]
             copies.append(send(theirs, theirs, z_dev(step)))
-            if side == min(part, 1):
+            if side == (0 if part == 1 else 1):
                 copies.append(send(theirs, theirs, z_dev(2 * step)))
         z_far[part] = copies
 
@@ -555,13 +554,14 @@
         last_copies[part] = send(mine, mine, sibling)
 
     x_start(0)
+    backward(*NEAR)
     x_start(1)
     y_copies = [
         send(part_of(1), y_in.at[0], y_dev(1)),
         send(part_of(-1), y_in.at[1], y_dev(-1)),
     ]
+    x_relay(0)
     backward(*FAR)
-    x_relay(0)
     x_start(2)
     y_relays = [
         send(part_of(3), y_relay.at[0], y_dev(1)),
@@ -650,15 +650,23 @@
     v_ref[...] = v_total
     store(v_ref, v_hbm)
 
+    def store_rows(which, part):
+        store(final.at[rows_of(which, part)], final_hbm.at[rows_of(which, part)])
+
+    def store_theirs(part):
+        last_copies[part].wait_recv()
+        store_rows(1 - core, part)
+
+    store_rows(core, 0)
     z_end(1)
+    store_rows(core, 1)
+    store_theirs(0)
     for copy in started[:early]:
         copy.wait_send()
     z_end(2)
-    for part in range(PARTS):
-        store(final.at[own_rows(part)], final_hbm.at[own_rows(part)])
-    for part in range(PARTS):
-        last_copies[part].wait_recv()
-        store(final.at[rows_of(1 - core, part)], final_hbm.at[rows_of(1 - core, part)])
+    store_rows(core, 2)
+    store_theirs(1)
+    store_theirs(2)
     for copy in started[early:]:
         copy.wait_send()
     for copy in stores:

time: 83.5 us -> 82.9 us (level)
  no operation moved by 1% of the time
where the time goes in v8:
time: 82.9 us; the launch traced here: 82.7 us
  Pallas kernels  82.1 us (99%)
    pallas_call x1, Pallas kernels, body(): pl.pallas_call(kernel, out_shape=(jax.ShapeDtypeStruct((rows, width), BF1...  79.3 us
    pallas_call x1, Pallas kernels, body(): pl.pallas_call(finish, out_shape=(jax.ShapeDtypeStruct((rows, width), BF1...  2.75 us

profile of v8, /device:TPU:1, one launch (start us, length us, event | category | flops | bytes accessed | tf_op | source)
XLA Modules:
  0.0 82.7 jit_solution(7480937388550225227)
XLA Ops:
  0.6 79.3 %shard_map.129 = (bf16[128,1024]{1,0:T(8,128)(2,1)}, bf16[1024,384]{1,0:T(8,128)(2,1)}, f32[1024,128]{1,0:T(8,128)}, f32[8,256]{1,0:T(8,128)}) custom-call(bf16[128,1024]{1,0:T(8,128)(2,1)} %bitcast.6, s32[1,128]{1,0:T(1,128)} %marks_hbm.1, bf16[8,128]{1,0:T(8,128)(2,1)} %bitcast.9, bf16[4,1024]{1,0:T(4,128)(2,1)} %conv_hbm.1, bf16[8,128]{1,0:T(8,128)(2,1)} %bitcast.10, ...), custom_call_target="tpu_custom_call" | custom-call | tf_op jit(solution)/shard_map/pallas_call | solution.py:786
  80.0 2.8 %shard_map.130 = (bf16[128,1024]{1,0:T(8,128)(2,1)}, f32[2048,128]{1,0:T(8,128)}, f32[2048,128]{1,0:T(8,128)}, f32[128,1024]{1,0:T(8,128)}) custom-call(bf16[128,1024]{1,0:T(8,128)(2,1)} %get-tuple-element.12.bg_hbm, bf16[1024,384]{1,0:T(8,128)(2,1)} %get-tuple-element.13.final_hbm, f32[1024,128]{1,0:T(8,128)} %get-tuple-element.14.tail_hbm, ...), custom_call_target="tpu_custom_call" | custom-call | tf_op jit(solution)/shard_map/pallas_call | solution.py:818

commit v9 on v8

--- a/solution.py
+++ b/solution.py
@@ -582,14 +582,15 @@
         send(v_out.at[2], v_in.at[1], x_dev(1)),
         send(v_out.at[3], v_in.at[2], x_dev(2)),
     ]
+    z_start(0)
     x_relay(2)
-    z_start(0)
 
     for copy in v_copies:
         copy.wait_recv()
     v_pair[...] = v_out[0] + v_in[0] + v_in[1] + v_in[2]
     v_swap = send(v_pair, v_sib, sibling)
 
+    z_sum(0)
     z_start(1)
     v_swap.wait_recv()
     v_all[z] = v_pair[...] + v_sib[...]
@@ -606,10 +607,9 @@
         y_mid[side, :, other] = total[:, other].astype(BF16)
         y_copies.append(send(y_mid.at[side], y_in.at[2 + side], y_dev(step)))
 
-    z_sum(0)
+    z_spread(0)
     z_start(2)
     z_sum(1)
-    z_spread(0)
     z_sum(2)
     z_spread(1)
     early = len(started)

time: 82.9 us -> 83.6 us (level)
  no operation moved by 1% of the time
where the time goes in v9:
time: 83.6 us; the launch traced here: 83.4 us
  Pallas kernels  82.8 us (99%)
    pallas_call x1, Pallas kernels, body(): pl.pallas_call(kernel, out_shape=(jax.ShapeDtypeStruct((rows, width), BF1...  80 us
    pallas_call x1, Pallas kernels, body(): pl.pallas_call(finish, out_shape=(jax.ShapeDtypeStruct((rows, width), BF1...  2.75 us

profile of v9, /device:TPU:1, one launch (start us, length us, event | category | flops | bytes accessed | tf_op | source)
XLA Modules:
  0.0 83.4 jit_solution(17008694909619015477)
XLA Ops:
  0.6 80.0 %shard_map.129 = (bf16[128,1024]{1,0:T(8,128)(2,1)}, bf16[1024,384]{1,0:T(8,128)(2,1)}, f32[1024,128]{1,0:T(8,128)}, f32[8,256]{1,0:T(8,128)}) custom-call(bf16[128,1024]{1,0:T(8,128)(2,1)} %bitcast.6, s32[1,128]{1,0:T(1,128)} %marks_hbm.1, bf16[8,128]{1,0:T(8,128)(2,1)} %bitcast.9, bf16[4,1024]{1,0:T(4,128)(2,1)} %conv_hbm.1, bf16[8,128]{1,0:T(8,128)(2,1)} %bitcast.10, ...), custom_call_target="tpu_custom_call" | custom-call | tf_op jit(solution)/shard_map/pallas_call | solution.py:786
  80.6 2.8 %shard_map.130 = (bf16[128,1024]{1,0:T(8,128)(2,1)}, f32[2048,128]{1,0:T(8,128)}, f32[2048,128]{1,0:T(8,128)}, f32[128,1024]{1,0:T(8,128)}) custom-call(bf16[128,1024]{1,0:T(8,128)(2,1)} %get-tuple-element.12.bg_hbm, bf16[1024,384]{1,0:T(8,128)(2,1)} %get-tuple-element.13.final_hbm, f32[1024,128]{1,0:T(8,128)} %get-tuple-element.14.tail_hbm, ...), custom_call_target="tpu_custom_call" | custom-call | tf_op jit(solution)/shard_map/pallas_call | solution.py:818

commit v10 on v8

--- a/solution.py
+++ b/solution.py
@@ -21,6 +21,8 @@
 Y_ROW = (0, 48, 96, 144, 192, 256, 304, 352)
 NEAR = (0, 240)
 FAR = (256, 400)
+THIRD = (256, 352)
+OPPOSITE = (352, 400)
 ROWS = 512
 X_ORDER = (0, -1, 1, 2)
 
@@ -316,9 +318,12 @@
             ring[which, side, direction, 2].wait_recv()
             pass_on(which, side, direction, 3)
 
+    def wait_third(which):
+        for side, direction in ((0, 1), (1, -1)):
+            ring[which, 1 - side, direction, 2].wait_recv()
+
     def wait_last(which):
         for side, direction in ((0, 1), (1, -1)):
-            ring[which, 1 - side, direction, 2].wait_recv()
             ring[which, side, direction, 3].wait_recv()
 
     relay(1, 1)
@@ -418,11 +423,15 @@
 
     lax.fori_loop(0, LINE, near_product, 0)
 
+    wait_third(1)
+    wait_third(0)
+    normalise(*THIRD)
+    forward(*THIRD, 0, LINE)
     wait_last(1)
     cot_t[1] = cot_all[FAR[0] : ROWS].T
     wait_last(0)
-    normalise(*FAR)
-    forward(*FAR, 0, LINE)
+    normalise(*OPPOSITE)
+    forward(*OPPOSITE, 0, LINE)
     normed_t[1] = normed[FAR[0] : ROWS].T
 
     def far_product(start, count, slot):
@@ -608,8 +617,8 @@
 
     z_sum(0)
     z_start(2)
+    z_spread(0)
     z_sum(1)
-    z_spread(0)
     z_sum(2)
     z_spread(1)
     early = len(started)

time: 82.9 us -> 84.5 us (1.019)
  Pallas kernels: 82.1 us -> 83.7 us
    pallas_call x1, Pallas kernels: 79.3 us -> 81 us  [body(): pl.pallas_call(kernel, out_shape=(jax.ShapeDtypeStruct((rows, width), BF1...]
where the time goes in v10:
time: 84.5 us; the launch traced here: 84.4 us
  Pallas kernels  83.7 us (99%)
    pallas_call x1, Pallas kernels, body(): pl.pallas_call(kernel, out_shape=(jax.ShapeDtypeStruct((rows, width), BF1...  81 us
    pallas_call x1, Pallas kernels, body(): pl.pallas_call(finish, out_shape=(jax.ShapeDtypeStruct((rows, width), BF1...  2.75 us

profile of v10, /device:TPU:1, one launch (start us, length us, event | category | flops | bytes accessed | tf_op | source)
XLA Modules:
  0.0 84.4 jit_solution(12637446890018697957)
XLA Ops:
  0.6 81.0 %shard_map.129 = (bf16[128,1024]{1,0:T(8,128)(2,1)}, bf16[1024,384]{1,0:T(8,128)(2,1)}, f32[1024,128]{1,0:T(8,128)}, f32[8,256]{1,0:T(8,128)}) custom-call(bf16[128,1024]{1,0:T(8,128)(2,1)} %bitcast.6, s32[1,128]{1,0:T(1,128)} %marks_hbm.1, bf16[8,128]{1,0:T(8,128)(2,1)} %bitcast.9, bf16[4,1024]{1,0:T(4,128)(2,1)} %conv_hbm.1, bf16[8,128]{1,0:T(8,128)(2,1)} %bitcast.10, ...), custom_call_target="tpu_custom_call" | custom-call | tf_op jit(solution)/shard_map/pallas_call | solution.py:795
  81.6 2.8 %shard_map.130 = (bf16[128,1024]{1,0:T(8,128)(2,1)}, f32[2048,128]{1,0:T(8,128)}, f32[2048,128]{1,0:T(8,128)}, f32[128,1024]{1,0:T(8,128)}) custom-call(bf16[128,1024]{1,0:T(8,128)(2,1)} %get-tuple-element.12.bg_hbm, bf16[1024,384]{1,0:T(8,128)(2,1)} %get-tuple-element.13.final_hbm, f32[1024,128]{1,0:T(8,128)} %get-tuple-element.14.tail_hbm, ...), custom_call_target="tpu_custom_call" | custom-call | tf_op jit(solution)/shard_map/pallas_call | solution.py:827
